TPU v7x, 32 devices: a whole 2x2x4 slice. The times are simulated.
32 devices in a mesh: groups: 2 (over y), dom: 16 (over z, x, core).
Axes of the slice: x: 2, y: 2, z: 4, core: 2. Of those that a mesh axis runs over, the one named last changes fastest.
Arguments:
- cartesian_places: float32 [3, 8192], P(None, ('groups', 'dom')), parts along dimension 1, may hold values from 0 to 16, as said below
- node_descriptors: bfloat16 [8192, 128], P(('groups', 'dom')), parts along dimension 0, may hold values from -12 to 12
- padded_partner_list: int32 [8192, 64], P(('groups', 'dom')), parts along dimension 0, may hold values from 0 to 383, as said below
- active_partner_number: int32 [8192], P(('groups', 'dom')), parts along dimension 0, may hold values from 32 to 64, as said below
- exported_site_indices: int32 [4096], P(('groups', 'dom')), parts along dimension 0, may hold values from 0 to 255, as said below
- fourier_modes: int32 [3, 12288], replicated, may hold values from -8 to 48, as said below
- hidden_pole_projection: bfloat16 [128, 16], replicated, may hold values from -0.5 to 0.5
- distance_mlp_first_matrix: bfloat16 [16, 128], replicated, may hold values from -1.5 to 1.5
- distance_mlp_second_matrix: bfloat16 [128, 128], replicated, may hold values from -0.5 to 0.5
- distance_mlp_final_matrix: bfloat16 [128, 128], replicated, may hold values from -0.5 to 0.5
- energy_projection: float32 [128], replicated, may hold values from -4 to 4
Outputs:
- forces: float32 [3, 8192], P(None, ('groups', 'dom')), parts along dimension 1
- feature_grad: bfloat16 [8192, 128], P(('groups', 'dom')), parts along dimension 0
There are 2 independent parts, one for each index of `groups`. A program takes and returns all parts, laid end to end along the dimension named above; an argument that names none is the same for every part. Nothing has to cross between parts.
Inputs may be any that keep to these rules, and one draw needn't show every extreme that they name: `cartesian_places`: atom a has x between a // 256 and a // 256 + 1; y and z lie between 0 and 4. `padded_partner_list`: slots in the numbering of the steps; entries past active_partner_number are padding. `active_partner_number`: the first atom of every domain has 64 live slots. `exported_site_indices`: the 128 entries of a domain are distinct local atom numbers; the first 64 go to the domain before, the others to the domain after. `fourier_modes`: distinct triples; the first component is 1 to 48, the others -8 to 7.
All inputs are finite; a program needn't handle non-finite values.
Results may differ from a plain program's by a relative error of at most 0.0034.
Values may be sent and summed in bfloat16 or wider, within the bound.
A program may use at most 64 MiB of HBM per device.

v0:
```python
import math

import jax
import jax.numpy as jnp
from jax import lax
from jax.sharding import PartitionSpec as P

CELL_SIDE = 4.0
PREC_HIGH = lax.Precision.HIGHEST
CONTRACT_FIRST = (((0,), (0,)), ((), ()))
CONTRACT_LAST = (((1,), (1,)), ((), ()))


def with_halo(block, sides, width):
    for axis, dim in sides:
        count = lax.axis_size(axis)
        forward = [(i, i + 1) for i in range(count - 1)]
        forward.append((count - 1, 0))
        backward = [(target, source) for source, target in forward]
        low = lax.ppermute(
            lax.slice_in_dim(block, block.shape[dim] - width, None, axis=dim), axis, forward
        )
        high = lax.ppermute(lax.slice_in_dim(block, 0, width, axis=dim), axis, backward)
        block = jnp.concatenate([low, block, high], axis=dim)
    return block


def decay_table(rate_count):
    return 0.02 * 64.0 ** (jnp.arange(rate_count, dtype=jnp.float32) / (rate_count - 1))


def silu_slope(values):
    logistic = jax.nn.sigmoid(values)
    return logistic * (1.0 + values * (1.0 - logistic))


def mode_lookup_array(fourier_modes, cubic_cell_side):
    lattice_sum_coefficients = jnp.array(
        [2.0 * math.pi / cubic_cell_side, 2.0 * math.pi / CELL_SIDE, 2.0 * math.pi / CELL_SIDE],
        jnp.float32,
    )
    fourier_space_modes = fourier_modes.astype(jnp.float32) * lattice_sum_coefficients[:, None]
    ksquare = jnp.sum(fourier_space_modes * fourier_space_modes, 0)
    mode_coefficient = 4.0 * jnp.exp(-ksquare / 1024.0) / (ksquare + 0.25)
    return (fourier_space_modes, mode_coefficient)


def phase_pair(coords, wave_part):
    phase_angle = (
        coords[0][:, None] * wave_part[0][None, :] + coords[1][:, None] * wave_part[1][None, :]
    )
    phase_angle = phase_angle + coords[2][:, None] * wave_part[2][None, :]
    return (jnp.cos(phase_angle), jnp.sin(phase_angle))


def edge_terms(
    separation,
    edge_mask,
    partner_feats,
    decay_rates,
    distance_mlp_first_matrix,
    distance_mlp_second_matrix,
    distance_mlp_final_matrix,
    energy_projection,
):
    atom_rows, slot_count = edge_mask.shape
    edge_total = atom_rows * slot_count
    edge_scale = slot_count ** (-0.5)
    squared = jnp.sum(separation * separation, 0).reshape(edge_total)
    radial_basis = jnp.exp(-decay_rates[:, None] * squared[None, :])
    pre_one = lax.dot_general(
        radial_basis.astype(jnp.bfloat16),
        distance_mlp_first_matrix,
        CONTRACT_FIRST,
        preferred_element_type=jnp.float32,
    )
    hidden_one = jax.nn.silu(pre_one).astype(jnp.bfloat16)
    pre_two = jnp.dot(hidden_one, distance_mlp_second_matrix, preferred_element_type=jnp.float32)
    hidden_two = jax.nn.silu(pre_two).astype(jnp.bfloat16)
    filters = jnp.dot(hidden_two, distance_mlp_final_matrix, preferred_element_type=jnp.float32)
    live_edges = edge_mask.reshape(edge_total, 1).astype(jnp.float32)
    feats_wide = partner_feats.astype(jnp.float32)
    weighted = live_edges * filters
    message = edge_scale * jnp.sum((weighted * feats_wide).reshape(atom_rows, slot_count, -1), 1)
    out_slope = energy_projection[None, :] * silu_slope(message)
    slope_edges = jnp.repeat(out_slope, slot_count, 0)
    filter_grad = (edge_scale * live_edges * slope_edges * feats_wide).astype(jnp.bfloat16)
    grad_two = lax.dot_general(
        filter_grad, distance_mlp_final_matrix, CONTRACT_LAST, preferred_element_type=jnp.float32
    )
    pre_grad_two = (grad_two * silu_slope(pre_two)).astype(jnp.bfloat16)
    grad_one = lax.dot_general(
        pre_grad_two, distance_mlp_second_matrix, CONTRACT_LAST, preferred_element_type=jnp.float32
    )
    pre_grad_one = (grad_one * silu_slope(pre_one)).astype(jnp.bfloat16)
    basis_grad = lax.dot_general(
        distance_mlp_first_matrix, pre_grad_one, CONTRACT_LAST, preferred_element_type=jnp.float32
    )
    square_grad = -jnp.sum(decay_rates[:, None] * radial_basis * basis_grad, 0)
    pair_grad = 2.0 * square_grad.reshape(atom_rows, slot_count)[None] * separation
    feat_grad = edge_scale * weighted * slope_edges
    return (pair_grad, feat_grad)


def long_factors(coords, charges, fourier_space_modes, kblock):
    number_of_modes = fourier_space_modes.shape[1]

    def factor_block(carry, block_index):
        first_wave = block_index * kblock
        wave_part = lax.dynamic_slice_in_dim(fourier_space_modes, first_wave, kblock, 1)
        cosines, sines = phase_pair(coords, wave_part)
        real_part = lax.dot_general(
            charges,
            cosines,
            CONTRACT_FIRST,
            precision=PREC_HIGH,
            preferred_element_type=jnp.float32,
        )
        imag_part = lax.dot_general(
            charges, sines, CONTRACT_FIRST, precision=PREC_HIGH, preferred_element_type=jnp.float32
        )
        return (carry, (real_part, imag_part))

    _, stacked = lax.scan(
        factor_block, None, jnp.arange(number_of_modes // kblock, dtype=jnp.int32)
    )
    real_all = stacked[0].transpose(1, 0, 2).reshape(charges.shape[1], number_of_modes)
    imag_all = stacked[1].transpose(1, 0, 2).reshape(charges.shape[1], number_of_modes)
    return (real_all, imag_all, None, None)


def long_backward(coords, charges, fourier_space_modes, real_grad, imag_grad, kblock):
    atom_count = coords.shape[1]

    def force_block(carry, block_index):
        force_acc, charge_acc = carry
        first_wave = block_index * kblock
        wave_part = lax.dynamic_slice_in_dim(fourier_space_modes, first_wave, kblock, 1)
        cosines, sines = phase_pair(coords, wave_part)
        real_slice = lax.dynamic_slice_in_dim(real_grad, first_wave, kblock, 1)
        imag_slice = lax.dynamic_slice_in_dim(imag_grad, first_wave, kblock, 1)
        along_real = jnp.dot(
            charges, real_slice, precision=PREC_HIGH, preferred_element_type=jnp.float32
        )
        along_imag = jnp.dot(
            charges, imag_slice, precision=PREC_HIGH, preferred_element_type=jnp.float32
        )
        dphase = cosines * along_imag - sines * along_real
        force_acc = force_acc + lax.dot_general(
            wave_part,
            dphase,
            CONTRACT_LAST,
            precision=PREC_HIGH,
            preferred_element_type=jnp.float32,
        )
        charge_acc = charge_acc + lax.dot_general(
            cosines,
            real_slice,
            CONTRACT_LAST,
            precision=PREC_HIGH,
            preferred_element_type=jnp.float32,
        )
        charge_acc = charge_acc + lax.dot_general(
            sines,
            imag_slice,
            CONTRACT_LAST,
            precision=PREC_HIGH,
            preferred_element_type=jnp.float32,
        )
        return ((force_acc, charge_acc), None)

    initial = (
        jnp.zeros((3, atom_count), jnp.float32),
        jnp.zeros((atom_count, real_grad.shape[0]), jnp.float32),
    )
    (force_acc, charge_acc), _ = lax.scan(
        force_block, initial, jnp.arange(real_grad.shape[1] // kblock, dtype=jnp.int32)
    )
    return (force_acc, charge_acc)


def local(
    cartesian_places,
    node_descriptors,
    padded_partner_list,
    active_partner_number,
    exported_site_indices,
    fourier_modes,
    hidden_pole_projection,
    distance_mlp_first_matrix,
    distance_mlp_second_matrix,
    distance_mlp_final_matrix,
    energy_projection,
):
    count_dom = lax.axis_size("dom")
    my_index = lax.axis_index("dom")
    atoms_here = node_descriptors.shape[0]
    feat_width = node_descriptors.shape[1]
    halo_rows = exported_site_indices.shape[0] // 2
    slot_count = padded_partner_list.shape[1]
    total_atoms = atoms_here * count_dom
    cubic_cell_side = float(count_dom)
    decay_rates = decay_table(distance_mlp_first_matrix.shape[0])
    outgoing = node_descriptors[exported_site_indices]
    widened = with_halo(outgoing, (("dom", 0),), halo_rows)
    halo_feats = jnp.concatenate([widened[:halo_rows], widened[3 * halo_rows :]], 0)
    out_coords = cartesian_places[:, exported_site_indices]
    wide_coords = with_halo(out_coords, (("dom", 1),), halo_rows)
    left_coords = wide_coords[:, :halo_rows]
    right_coords = wide_coords[:, 3 * halo_rows :]
    left_coords = left_coords.at[0].add(
        jnp.where(my_index == 0, -cubic_cell_side, 0.0).astype(jnp.float32)
    )
    right_coords = right_coords.at[0].add(
        jnp.where(my_index == count_dom - 1, cubic_cell_side, 0.0).astype(jnp.float32)
    )
    table_feats = jnp.concatenate([node_descriptors, halo_feats], 0)
    table_coords = jnp.concatenate([cartesian_places, left_coords, right_coords], 1)
    atom_block = math.gcd(atoms_here, max(1, 1024 // slot_count))
    slot_ids = jnp.arange(slot_count, dtype=jnp.int32)

    def edge_block(carry, block_index):
        grad_pos, grad_feat = carry
        first_row = block_index * atom_block
        owners = first_row + jnp.arange(atom_block, dtype=jnp.int32)
        nbr_slots = lax.dynamic_slice_in_dim(padded_partner_list, first_row, atom_block, 0)
        counts = lax.dynamic_slice_in_dim(active_partner_number, first_row, atom_block, 0)
        own_coords = lax.dynamic_slice_in_dim(cartesian_places, first_row, atom_block, 1)
        near = table_coords[:, nbr_slots]
        separation = near - own_coords[:, :, None]
        edge_mask = slot_ids[None, :] < counts[:, None]
        slot_flat = nbr_slots.reshape(-1)
        pair_grad, feat_grad = edge_terms(
            separation,
            edge_mask,
            table_feats[slot_flat],
            decay_rates,
            distance_mlp_first_matrix,
            distance_mlp_second_matrix,
            distance_mlp_final_matrix,
            energy_projection,
        )
        grad_pos = grad_pos.at[:, slot_flat].add(pair_grad.reshape(3, -1))
        grad_pos = grad_pos.at[:, owners].add(-jnp.sum(pair_grad, 2))
        grad_feat = grad_feat.at[slot_flat].add(feat_grad)
        return ((grad_pos, grad_feat), None)

    table_rows = atoms_here + 2 * halo_rows
    initial = (
        jnp.zeros((3, table_rows), jnp.float32),
        jnp.zeros((table_rows, feat_width), jnp.float32),
    )
    (grad_pos, grad_feat), _ = lax.scan(
        edge_block, initial, jnp.arange(atoms_here // atom_block, dtype=jnp.int32)
    )
    returned = with_halo(grad_feat[atoms_here:], (("dom", 0),), halo_rows)
    returned = jnp.concatenate([returned[:halo_rows], returned[3 * halo_rows :]], 0)
    returned_pos = with_halo(grad_pos[:, atoms_here:], (("dom", 1),), halo_rows)
    returned_pos = jnp.concatenate(
        [returned_pos[:, :halo_rows], returned_pos[:, 3 * halo_rows :]], 1
    )
    short_feat = grad_feat[:atoms_here].at[exported_site_indices].add(returned)
    short_grad = grad_pos[:, :atoms_here].at[:, exported_site_indices].add(returned_pos)
    fourier_space_modes, mode_coefficient = mode_lookup_array(fourier_modes, cubic_cell_side)
    number_of_modes = fourier_modes.shape[1]
    coupling = float(total_atoms * number_of_modes) ** (-0.5)
    kblock = math.gcd(number_of_modes, 512)
    charges_raw = jnp.dot(
        node_descriptors, hidden_pole_projection, preferred_element_type=jnp.float32
    )
    charge_sums = lax.psum(jnp.sum(charges_raw, 0), "dom")
    charges = charges_raw - charge_sums / total_atoms
    real_sf, imag_sf, unused_cos, unused_sin = long_factors(
        cartesian_places, charges, fourier_space_modes, kblock
    )
    real_sf, imag_sf = lax.psum((real_sf, imag_sf), "dom")
    real_grad = 2.0 * coupling * mode_coefficient[None, :] * real_sf
    imag_grad = 2.0 * coupling * mode_coefficient[None, :] * imag_sf
    long_grad, charge_grad = long_backward(
        cartesian_places, charges, fourier_space_modes, real_grad, imag_grad, kblock
    )
    grad_mean = lax.psum(jnp.sum(charge_grad, 0), "dom") / total_atoms
    raw_grad = charge_grad - grad_mean
    feat_long = jnp.dot(
        raw_grad,
        hidden_pole_projection.astype(jnp.float32).T,
        precision=PREC_HIGH,
        preferred_element_type=jnp.float32,
    )
    forces = -(short_grad + long_grad)
    feature_grad = (short_feat + feat_long).astype(jnp.bfloat16)
    return (forces, feature_grad)


def solution(mesh):
    in_specs = (
        P(None, ("groups", "dom")),
        P(("groups", "dom"), None),
        P(("groups", "dom"), None),
        P(("groups", "dom")),
        P(("groups", "dom")),
        P(),
        P(),
        P(),
        P(),
        P(),
        P(),
    )
    out_specs = (P(None, ("groups", "dom")), P(("groups", "dom"), None))
    return jax.shard_map(local, mesh=mesh, in_specs=in_specs, out_specs=out_specs, check_vma=False)
```

profile of v0, /device:TPU:0, one launch (start us, length us, event | category | flops | bytes accessed | tf_op | source)
XLA Modules:
  0.0 995.3 jit_solution(17952952137773576336)
XLA Ops:
  9.3 5.5 collective-permute-start.1
  15.5 4.5 collective-permute-start.3
  20.2 33.9 %psum.28 = f32[16]{0:T(128)S(1)} all-reduce(f32[16]{0:T(128)S(1)} %get-tuple-element.458), channel_id=1, replica_groups=mesh['groups'=2,'dom'=16] {'dom'}, use_global_device_ids=true, to_apply=%region_11.12 | all-reduce | flops 16 | bytes 128 | tf_op jit(solution)/shard_map/psum | solution.py:271
  55.7 141.7 %while.41 = (s32[]{:T(128)}, f32[24,16,512]{2,1,0:T(8,128)S(1)}, f32[24,16,512]{2,1,0:T(8,128)S(1)}, f32[3,256]{1,0:T(4,128)S(1)}, s32[24]{0:T(128)S(1)}, /*inde...) while((s32[]{:T(128)}, f32[24,16,512]{2,1,0:T(8,128)S(1)}, ...), condition=%wide.region_13.14_spmd, body=%wide.region_12.13_spmd.sunk | while | flops 51642376 | bytes 135403 | solution.py:124
  202.1 477.5 %while.42 = (s32[]{:T(128)}, f32[3,384]{0,1:T(8,128)S(1)}, f32[384,128]{1,0:T(8,128)S(1)}, s32[16]{0:T(128)S(1)}, s32[256,64]{1,0:T(8,128)S(1)}, /*index=5*/f32[...) while((s32[]{:T(128)}, f32[3,384]{0,1:T(8,128)S(1)}, ...), condition=%wide.region_8.9_spmd.clone, body=%wide.region_0.8_spmd.clone.sunk | while | flops 147866816 | bytes 11979187 | solution.py:253
  217.9 6.2 scatter_custom_fusion.18
  225.2 6.1 scatter_fusion
  247.7 6.2 scatter_custom_fusion.18
  255.0 6.1 scatter_fusion
  266.9 3.2 gather_fusion.1
  277.6 6.2 scatter_custom_fusion.18
  284.9 6.1 scatter_fusion
  296.7 3.2 gather_fusion.1
  307.4 6.2 scatter_custom_fusion.18
  314.7 6.1 scatter_fusion
  337.3 6.2 scatter_custom_fusion.18
  344.5 6.1 scatter_fusion
  367.1 6.2 scatter_custom_fusion.18
  374.4 6.1 scatter_fusion
  397.0 6.2 scatter_custom_fusion.18
  404.2 6.1 scatter_fusion
  416.1 3.2 gather_fusion.1
  426.8 6.2 scatter_custom_fusion.18
  434.1 6.1 scatter_fusion
  456.7 6.2 scatter_custom_fusion.18
  463.9 6.1 scatter_fusion
  475.8 3.2 gather_fusion.1
  486.5 6.2 scatter_custom_fusion.18
  493.8 6.1 scatter_fusion
  505.6 3.2 gather_fusion.1
  516.4 6.2 scatter_custom_fusion.18
  523.6 6.1 scatter_fusion
  535.5 3.2 gather_fusion.1
  546.2 6.2 scatter_custom_fusion.18
  553.5 6.1 scatter_fusion
  576.0 6.2 scatter_custom_fusion.18
  583.3 6.1 scatter_fusion
  595.2 3.2 gather_fusion.1
  605.9 6.2 scatter_custom_fusion.18
  613.1 6.1 scatter_fusion
  625.0 3.2 gather_fusion.1
  635.7 6.2 scatter_custom_fusion.18
  643.0 6.1 scatter_fusion
  665.6 6.2 scatter_custom_fusion.18
  672.8 6.1 scatter_fusion
  680.4 4.0 collective-permute-start.7
  687.2 263.2 %while.43 = (s32[]{:T(128)}, f32[3,256]{1,0:T(4,128)S(1)}, f32[256,16]{0,1:T(8,128)S(1)}, s32[24]{0:T(128)S(1)}, f32[3,12288]{1,0:T(4,128)S(1)}, /*index=5*/f32[...) while((s32[]{:T(128)}, f32[3,256]{1,0:T(4,128)S(1)}, ...), condition=%wide.region_17.18_spmd.clone, body=%wide.region_16.17_spmd.clone.sunk | while | flops 108410376 | bytes 2397458 | solution.py:176
  950.6 32.8 %psum.31 = f32[16]{0:T(128)S(1)} all-reduce(f32[16]{0:T(128)S(1)} %reduce_sum.69), channel_id=1, replica_groups=mesh['groups'=2,'dom'=16] {'dom'}, use_global_device_ids=true, to_apply=%region_20.21 | all-reduce | flops 16 | bytes 128 | tf_op jit(solution)/shard_map/psum | solution.py:282
  (1261 shorter events, 629.6 us)
Async XLA Ops:
  7.2 12.8 %copy-start = (bf16[128,16]{0,1:T(8,128)(2,1)S(1)}, bf16[128,16]{0,1:T(8,128)(2,1)}, u32[]{:S(2)}) copy-start(bf16[128,16]{0,1:T(8,128)(2,1)} %param.28) | copy-start | bytes 12292
  7.2 678.4 %all-reduce.3.cloned.1.call-start = ((), (), s32[]{:S(2)}) async-start(), calls=%async_computation | async-start | bytes 3145728 | tf_op jit(solution)/shard_map/psum | solution.py:276
  9.3 5.5 copy-start.1
  9.3 191.0 %collective-permute-start.1 = (f32[3,64]{0,1:T(8,128)S(1)}, f32[3,64]{0,1:T(8,128)S(1)}, u32[]{:S(2)}, u32[]{:S(2)}) collective-permute-start(f32[3,64]{0,1:T(8,128)S(1)} %get-tuple-element.451), channel_id=1, source_target_pairs={{1,0},{2,1},{3,2},{4,3},{5,4},{6,5},{7,6},{8,7},{9,8},{10,9},{11,1... | collective-permute-start | bytes 2312 | tf_op jit(solution)/shard_map/ppermute | solution.py:23
  14.8 39.4 %copy-start.3 = (s32[3,12288]{1,0:T(4,128)S(1)}, s32[3,12288]{1,0:T(4,128)}, u32[]{:S(2)}) copy-start(s32[3,12288]{1,0:T(4,128)} %param.27) | copy-start | bytes 442372
  14.8 185.8 %collective-permute-start = (f32[3,64]{0,1:T(8,128)S(1)}, f32[3,64]{0,1:T(8,128)S(1)}, u32[]{:S(2)}, u32[]{:S(2)}) collective-permute-start(f32[3,64]{0,1:T(8,128)S(1)} %get-tuple-element.450), channel_id=1, source_target_pairs={{0,1},{1,2},{2,3},{3,4},{4,5},{5,6},{6,7},{7,8},{8,9},{9,10},{10,1... | collective-permute-start | bytes 2312 | tf_op jit(solution)/shard_map/ppermute | solution.py:20
  15.5 185.8 %collective-permute-start.3 = (bf16[64,128]{1,0:T(8,128)(2,1)S(1)}, bf16[64,128]{1,0:T(8,128)(2,1)S(1)}, u32[]{:S(2)}, u32[]{:S(2)}) collective-permute-start(bf16[64,128]{1,0:T(8,128)(2,1)S(1)} %get-tuple-element.455), channel_id=1, source_target_pairs={{1,0},{2,1},{3,2},{4,3},{5,4},{6,5},{7,6},{8,7},{9,8},{10,9},{11,1... | collective-permute-start | bytes 49160 | tf_op jit(solution)/shard_map/ppermute | solution.py:23
  20.0 181.3 %collective-permute-start.2 = (bf16[64,128]{1,0:T(8,128)(2,1)S(1)}, bf16[64,128]{1,0:T(8,128)(2,1)S(1)}, u32[]{:S(2)}, u32[]{:S(2)}) collective-permute-start(bf16[64,128]{1,0:T(8,128)(2,1)S(1)} %get-tuple-element.454), channel_id=1, source_target_pairs={{0,1},{1,2},{2,3},{3,4},{4,5},{5,6},{6,7},{7,8},{8,9},{9,10},{10,1... | collective-permute-start | bytes 49160 | tf_op jit(solution)/shard_map/ppermute | solution.py:20
  211.1 2.0 copy-start.18
  215.2 1.1 copy-start.23
  225.1 6.2 copy-start.17
  240.9 2.0 copy-start.18
  255.0 6.2 copy-start.17
  270.8 2.0 copy-start.18
  284.8 6.2 copy-start.17
  300.6 2.0 copy-start.18
  314.7 6.2 copy-start.17
  330.5 2.0 copy-start.18
  344.5 6.2 copy-start.17
  360.3 2.0 copy-start.18
  374.4 6.2 copy-start.17
  390.1 2.0 copy-start.18
  404.2 6.2 copy-start.17
  420.0 2.0 copy-start.18
  434.1 6.2 copy-start.17
  449.8 2.0 copy-start.18
  463.9 6.2 copy-start.17
  479.7 2.0 copy-start.18
  493.8 6.2 copy-start.17
  509.5 2.0 copy-start.18
  523.6 6.2 copy-start.17
  539.4 2.0 copy-start.18
  553.4 6.2 copy-start.17
  569.2 2.0 copy-start.18
  583.3 6.2 copy-start.17
  599.1 2.0 copy-start.18
  613.1 6.2 copy-start.17
  628.9 2.0 copy-start.18
  633.0 1.1 copy-start.23
  643.0 6.2 copy-start.17
  658.7 2.0 copy-start.18
  672.8 6.2 copy-start.17
  679.8 4.6 collective-permute-start.5
  679.8 5.8 collective-permute-start.4
  680.3 5.3 copy-start.4
  680.4 306.0 %collective-permute-start.7 = (f32[64,128]{1,0:T(8,128)S(1)}, f32[64,128]{1,0:T(8,128)S(1)}, u32[]{:S(2)}, u32[]{:S(2)}) collective-permute-start(f32[64,128]{1,0:T(8,128)S(1)} %get-tuple-element.449), channel_id=1, source_target_pairs={{1,0},{2,1},{3,2},{4,3},{5,4},{6,5},{7,6},{8,7},{9,8},{10,9},{11,1... | collective-permute-start | bytes 98312 | tf_op jit(solution)/shard_map/ppermute | solution.py:23
  684.4 302.0 %collective-permute-start.6 = (f32[64,128]{1,0:T(8,128)S(1)}, f32[64,128]{1,0:T(8,128)S(1)}, u32[]{:S(2)}, u32[]{:S(2)}) collective-permute-start(f32[64,128]{1,0:T(8,128)S(1)} %get-tuple-element.448), channel_id=1, source_target_pairs={{0,1},{1,2},{2,3},{3,4},{4,5},{5,6},{6,7},{7,8},{8,9},{9,10},{10,1... | collective-permute-start | bytes 98312 | tf_op jit(solution)/shard_map/ppermute | solution.py:20
  685.6 1.5 copy-start.8
  (150 other events, 106.7 us)
Sparse Core Ops, SparseCore 0:
  199.5 93.0 all-reduce.2
where the time goes:
time: 999 us; the launch traced here: 995 us
  matrix products  394 us (39%)
  other arithmetic  232 us (23%)
  local copies, waits for them, and re-layouts  225 us (23%)
  blocking collectives  66.7 us (7%)
  loops' own time  48.2 us (5%)
  starting transfers between devices  14.5 us (1%)
  between operations  14.4 us (1%)
    scatter-add x16, other arithmetic, edge_block(): grad_pos = grad_pos.at[:, slot_flat].add(pair_grad.reshape(3, -1))  98.6 us
    scatter-add x16, other arithmetic, edge_block(): grad_feat = grad_feat.at[slot_flat].add(feat_grad)  98 us
    dot_general x24, matrix products, force_block(): jnp.dot(charges, real_slice, precision=PREC_HIGH, preferred_element_type=...  58 us
    while x352, local copies, waits for them, and re-layouts  57.9 us
    dot_general x24, matrix products, force_block(): jnp.dot(charges, imag_slice, precision=PREC_HIGH, preferred_element_type=...  57 us
    dot_general x24, matrix products, factor_block(): lax.dot_general(charges, sines, CONTRACT_FIRST, precision=PREC_HIGH, pref...  54.9 us
    dot_general x24, matrix products, factor_block(): lax.dot_general(charges, cosines, CONTRACT_FIRST, precision=PREC_HIGH, pr...  54.4 us
    dot_general x24, matrix products, force_block(): lax.dot_general(cosines, real_slice, CONTRACT_LAST, precision=PREC_HIGH,...  53.7 us
  transfers between devices with their start and end apart: 9, of which 1 were waited for; matrix products, arithmetic and copies ran while one was open for 79% of the time, Pallas kernels for 0%

commit v1 on v0

v1 whole, which is shorter than its diff:
```python
import functools
import math

import jax
import jax.numpy as jnp
from jax import lax
from jax.experimental import pallas as pl
from jax.experimental.pallas import tpu as pltpu
from jax.sharding import PartitionSpec as P

CELL_SIDE = 4.0
PREC_HIGH = lax.Precision.HIGHEST
F32 = jnp.float32
BF16 = jnp.bfloat16
NT = (((1,), (1,)), ((), ()))
NN = (((1,), (0,)), ((), ()))
TN = (((0,), (0,)), ((), ()))
MODES_X = 48
MODES_Y = 16
MODES_Z = 16


def dotf(a, b, dims=NN):
    return lax.dot_general(a, b, dims, preferred_element_type=F32)


def split2(a):
    hi = a.astype(BF16)
    return hi, (a - hi.astype(F32)).astype(BF16)


def split3(a):
    hi = lax.reduce_precision(a, 8, 7)
    mid = lax.reduce_precision(a - hi, 8, 7)
    return hi.astype(BF16), mid.astype(BF16), (a - hi - mid).astype(BF16)


def dot3(a, b, dims):
    ah, al = a
    bh, bl = b
    return dotf(ah, bh, dims) + (dotf(al, bh, dims) + dotf(ah, bl, dims))


def sincos_turns(turns):
    x = (turns - jnp.round(turns)) * (2.0 * math.pi)
    x2 = x * x
    c = jnp.full_like(x, 1.0 / math.factorial(16))
    for n in range(14, -1, -2):
        c = c * x2 + (-1.0) ** (n // 2) / math.factorial(n)
    s = jnp.full_like(x, 1.0 / math.factorial(17))
    for n in range(15, 0, -2):
        s = s * x2 + (-1.0) ** (n // 2) / math.factorial(n)
    return c, s * x


def edge_kernel(slots, idx_ref, table_ref, own_ref, w1t_ref, w1_ref, w2t_ref, w2_ref, w3t_ref, w3_ref, eproj_ref, decay_ref, acc_ref, own_out_ref):
    edges = idx_ref.shape[2]
    atoms = own_ref.shape[2]
    rows = table_ref.shape[1]
    scale = slots ** (-0.5)
    chan = w3t_ref.shape[0]

    @pl.when(pl.program_id(0) == 0)
    def _():
        acc_ref[...] = jnp.zeros_like(acc_ref)

    idx = idx_ref[0]
    one = jnp.where(lax.broadcasted_iota(jnp.int32, (rows, edges), 0) == idx, 1.0, 0.0).astype(BF16)
    first = lax.broadcasted_iota(jnp.int32, (atoms, edges), 0) * slots
    edge_id = lax.broadcasted_iota(jnp.int32, (atoms, edges), 1)
    owner = jnp.where((edge_id >= first) & (edge_id < first + slots), 1.0, 0.0).astype(BF16)
    got = dotf(table_ref[...], one)
    feats = got[:chan]
    own = dotf(own_ref[0], owner)
    sep = got[chan : chan + 8]
    sep = sep - own[0:8]
    for n in (8, 16):
        sep = sep + (got[chan + n : chan + n + 8] - own[n : n + 8])
    sep = sep + got[chan + 24 : chan + 32]
    sq = jnp.sum(sep * sep, 0, keepdims=True)
    decay = decay_ref[...]
    basis = jnp.exp(-decay * sq)
    pre1 = dotf(w1t_ref[...], basis.astype(BF16))
    sig1 = 0.5 * jnp.tanh(0.5 * pre1) + 0.5
    h1 = pre1 * sig1
    slope1 = sig1 + h1 * (1.0 - sig1)
    pre2 = dotf(w2t_ref[...], h1.astype(BF16))
    sig2 = 0.5 * jnp.tanh(0.5 * pre2) + 0.5
    h2 = pre2 * sig2
    slope2 = sig2 + h2 * (1.0 - sig2)
    filters = dotf(w3t_ref[...], h2.astype(BF16))
    prod_hi, prod_lo = split2(filters * feats)
    message = scale * (dotf(prod_hi, owner, NT) + dotf(prod_lo, owner, NT))
    sigm = 1.0 / (1.0 + jnp.exp(-message))
    out_slope = scale * eproj_ref[...] * (sigm * (1.0 + message * (1.0 - sigm)))
    os_hi, os_lo = split2(out_slope)
    slope_e = dotf(os_hi, owner) + dotf(os_lo, owner)
    fgrad = (slope_e * feats).astype(BF16)
    g2 = (dotf(w3_ref[...], fgrad) * slope2).astype(BF16)
    g1 = (dotf(w2_ref[...], g2) * slope1).astype(BF16)
    bg = dotf(w1_ref[...], g1)
    sgrad = -2.0 * jnp.sum(decay * basis * bg, 0, keepdims=True)
    pair = sgrad * sep
    pair_hi, pair_lo = split2(pair)
    pairs = jnp.concatenate([pair_hi, pair_lo], 0)
    acc_ref[0:chan, :] += dotf((filters * slope_e).astype(BF16), one, NT)
    acc_ref[chan:, :] += dotf(pairs, one, NT)
    own_out_ref[0] = dotf(pairs, owner, NT)


def long_kernel(nk, inv_side, data_ref, mean_ref, kp_ref, wave_ref, wt_ref, out_ref, sf_ref, mh_ref, ml_ref):
    phase = pl.program_id(0)
    block = pl.program_id(1)
    mp = kp_ref.shape[1]
    chan = mean_ref.shape[0]
    nb = data_ref.shape[1]
    q = data_ref[0:chan, :] - mean_ref[...]
    x = data_ref[chan : chan + 1, :] * inv_side
    y = data_ref[chan + 1 : chan + 2, :] * (1.0 / CELL_SIDE)
    z = data_ref[chan + 2 : chan + 3, :] * (1.0 / CELL_SIDE)
    ec, es = sincos_turns(kp_ref[0] * x + kp_ref[1] * y)
    k2 = lax.broadcasted_iota(jnp.int32, (MODES_Z, 1), 0).astype(F32) - float(MODES_Z // 2)
    zc, zs = sincos_turns(k2 * z)
    half = chan * MODES_Z
    a_re = (q[:, None, :] * zc[None, :, :]).reshape(half, nb)
    a_im = (q[:, None, :] * zs[None, :, :]).reshape(half, nb)
    acat = split2(jnp.concatenate([a_re, a_im], 0))
    ecat = split2(jnp.concatenate([ec, es], 0))

    @pl.when((phase == 0) & (block == 0))
    def _():
        sf_ref[...] = jnp.zeros_like(sf_ref)

    @pl.when(phase == 0)
    def _():
        sf_ref[...] += dot3(acat, ecat, NT)

    @pl.when((phase == 0) & (block == nk - 1))
    def _():
        s = sf_ref[...]
        wt = wt_ref[...]
        re = wt * (s[:half, :mp] - s[half:, mp:])
        im = wt * (s[:half, mp:] + s[half:, :mp])
        m = jnp.concatenate(
            [jnp.concatenate([re, im], 1), jnp.concatenate([im, -re], 1)], 0
        )
        hi, lo = split2(m)
        mh_ref[...] = hi
        ml_ref[...] = lo

    @pl.when(phase == 1)
    def _():
        m = (mh_ref[...], ml_ref[...])
        u = dot3(m, ecat, NN)
        ur = u[:half].reshape(chan, MODES_Z, nb)
        ui = u[half:].reshape(chan, MODES_Z, nb)
        cg = jnp.sum(zc[None] * ur + zs[None] * ui, 1)
        kz = k2 * (2.0 * math.pi / CELL_SIDE)
        lz = jnp.sum((kz * zc)[None] * ui - (kz * zs)[None] * ur, 1)
        lz = jnp.sum(q * lz, 0, keepdims=True)
        p = dot3(m, acat, TN)
        dp = ec * p[mp:] - es * p[:mp]
        lx = jnp.sum(wave_ref[0] * dp, 0, keepdims=True)
        ly = jnp.sum(wave_ref[1] * dp, 0, keepdims=True)
        out_ref[0:chan, :] = cg
        out_ref[chan:, :] = jnp.concatenate([lx, ly, lz, jnp.zeros((5, nb), F32)], 0)


def long_range(places, nodes_t, proj, side, modes):
    n = lax.axis_size("dom")
    here = places.shape[1]
    chan = proj.shape[1]
    total = n * here
    raw = dotf(proj.T, nodes_t)
    mine = jnp.concatenate([raw, places, jnp.zeros((5, here), F32)], 0)
    data = lax.all_gather(mine, "dom", axis=1, tiled=True)
    mean = jnp.sum(data[:chan], 1, keepdims=True) / total
    pairs = MODES_X * MODES_Y
    m = -(-pairs // n)
    mp = -(-m // 8) * 8
    local_p = jnp.arange(mp, dtype=jnp.int32)
    flat = lax.axis_index("dom") * m + local_p
    real = (local_p < m) & (flat < pairs)
    k0 = (flat // MODES_Y + 1).astype(F32)
    k1 = (flat % MODES_Y - MODES_Y // 2).astype(F32)
    kx, ky = k0 * (2.0 * math.pi / side), k1 * (2.0 * math.pi / CELL_SIDE)
    kz = (jnp.arange(MODES_Z) - MODES_Z // 2).astype(F32) * (2.0 * math.pi / CELL_SIDE)
    ksq = (kx * kx + ky * ky)[None, :] + (kz * kz)[:, None]
    coupling = float(total * modes) ** (-0.5)
    wt = 2.0 * coupling * 4.0 * jnp.exp(-ksq / 1024.0) / (ksq + 0.25)
    wt = jnp.where(real[None, :], wt, 0.0)
    wt = jnp.tile(wt, (chan, 1))
    kp = jnp.stack([k0, k1])[:, :, None]
    wave = jnp.stack([kx, ky])[:, :, None]
    nb = math.gcd(total, 512)
    nk = total // nb
    half = chan * MODES_Z
    whole = lambda shape: pl.BlockSpec(shape, lambda a, b: (0,) * len(shape))
    rows = data.shape[0]
    out = pl.pallas_call(
        functools.partial(long_kernel, nk, 1.0 / side),
        out_shape=jax.ShapeDtypeStruct((rows, total), F32),
        grid=(2, nk),
        in_specs=[
            pl.BlockSpec((rows, nb), lambda a, b: (0, b)),
            whole((chan, 1)),
            whole((2, mp, 1)),
            whole((2, mp, 1)),
            whole((half, mp)),
        ],
        out_specs=pl.BlockSpec((rows, nb), lambda a, b: (0, a * b)),
        scratch_shapes=[
            pltpu.VMEM((2 * half, 2 * mp), F32),
            pltpu.VMEM((2 * half, 2 * mp), BF16),
            pltpu.VMEM((2 * half, 2 * mp), BF16),
        ],
        compiler_params=pltpu.CompilerParams(vmem_limit_bytes=40 * 2**20),
        cost_estimate=pl.CostEstimate(flops=4 * 10**9, bytes_accessed=2 * 10**6, transcendentals=0),
        name="long_range",
    )(data, mean, kp, wave, wt)
    sums = jnp.sum(out[:chan], 1)
    line = jnp.tile(jnp.pad(sums, (0, here - chan)), n)[None]
    out = jnp.concatenate([out[: chan + 3], line, out[chan + 4 :]], 0)
    mine = lax.psum_scatter(out, "dom", scatter_dimension=1, tiled=True)
    charge_grad = mine[:chan]
    raw_grad = charge_grad - mine[chan + 3, :chan][:, None] / total
    return mine[chan : chan + 3], raw_grad


def shift_pair(to_prev, to_next):
    n = lax.axis_size("dom")
    forward = [(i, (i + 1) % n) for i in range(n)]
    backward = [(t, s) for s, t in forward]
    from_prev = lax.ppermute(to_next, "dom", forward)
    from_next = lax.ppermute(to_prev, "dom", backward)
    return from_prev, from_next


def local(places, nodes, partners, counts, exported, modes, proj, w1, w2, w3, eproj):
    n = lax.axis_size("dom")
    me = lax.axis_index("dom")
    here, chan = nodes.shape
    halo = exported.shape[0] // 2
    slots = partners.shape[1]
    side = float(n)
    nrbf = w1.shape[0]
    nodes_t = nodes.T

    pad8 = lambda a: jnp.pad(a, ((0, 5), (0, 0)))
    parts = jnp.concatenate([pad8(a) for a in split3(places)], 0)
    mine = jnp.concatenate([nodes_t, parts], 0)
    pick = (jnp.arange(here, dtype=jnp.int32)[:, None] == exported[None, :]).astype(BF16)
    sent = dotf(mine, pick).astype(BF16)
    left, right = shift_pair(sent[:, :halo], sent[:, halo:])
    table = jnp.concatenate([mine, left, right], 1)
    col = jnp.arange(here + 2 * halo)
    shift = jnp.where((col >= here) & (col < here + halo) & (me == 0), -side, 0.0)
    shift = shift + jnp.where((col >= here + halo) & (me == n - 1), side, 0.0)
    table = jnp.concatenate([table, jnp.pad(shift[None].astype(BF16), ((0, 7), (0, 0)))], 0)

    long_grad, raw_grad = long_range(places, nodes_t, proj, side, modes.shape[1])

    blk = math.gcd(here, 32)
    nblk = here // blk
    edges = blk * slots
    live = jnp.arange(slots, dtype=jnp.int32)[None, :] < counts[:, None]
    idx = jnp.where(live, partners, -1).reshape(nblk, 1, edges)
    own = parts.reshape(24, nblk, blk).transpose(1, 0, 2)
    decay = (0.02 * 64.0 ** (jnp.arange(nrbf, dtype=F32) / (nrbf - 1)))[:, None]
    rows = table.shape[1]
    whole = lambda a: pl.BlockSpec(a.shape, lambda i: (0,) * a.ndim)
    fixed = [w1.T, w1, w2.T, w2, w3.T, w3, eproj[:, None], decay]
    acc, own_out = pl.pallas_call(
        functools.partial(edge_kernel, slots),
        out_shape=(
            jax.ShapeDtypeStruct((chan + 16, rows), F32),
            jax.ShapeDtypeStruct((nblk, 16, blk), F32),
        ),
        grid=(nblk,),
        in_specs=[
            pl.BlockSpec((1, 1, edges), lambda i: (i, 0, 0)),
            whole(table),
            pl.BlockSpec((1, 24, blk), lambda i: (i, 0, 0)),
        ]
        + [whole(a) for a in fixed],
        out_specs=(
            pl.BlockSpec((chan + 16, rows), lambda i: (0, 0)),
            pl.BlockSpec((1, 16, blk), lambda i: (i, 0, 0)),
        ),
        compiler_params=pltpu.CompilerParams(vmem_limit_bytes=48 * 2**20),
        cost_estimate=pl.CostEstimate(flops=8 * 10**9, bytes_accessed=2 * 10**6, transcendentals=0),
        name="edges",
    )(idx, table, own, *fixed)
    own_sum = own_out.transpose(1, 0, 2).reshape(16, here)
    grads = jnp.concatenate([acc[:chan], acc[chan : chan + 8] + acc[chan + 8 :]], 0)
    back_left, back_right = shift_pair(grads[:, here : here + halo], grads[:, here + halo :])
    returned = jnp.concatenate([back_left, back_right], 1)
    return finish(grads, returned, own_sum, pick, long_grad, raw_grad, proj, here, chan)


def finish(grads, returned, own_sum, pick, long_grad, raw_grad, proj, here, chan):
    back = lax.dot_general(returned, pick.astype(F32), NT, precision=PREC_HIGH, preferred_element_type=F32)
    grads = grads[:, :here] + back
    short_grad = grads[chan : chan + 3] - own_sum[0:3] - own_sum[8:11]
    forces = -(short_grad + long_grad)
    feat_long = lax.dot_general(proj.astype(F32), raw_grad, NN, precision=PREC_HIGH, preferred_element_type=F32)
    feature_grad = (grads[:chan] + feat_long).T.astype(BF16)
    return (forces, feature_grad)


def solution(mesh):
    both = ("groups", "dom")
    in_specs = (P(None, both), P(both, None), P(both, None), P(both), P(both)) + (P(),) * 6
    out_specs = (P(None, both), P(both, None))
    return jax.shard_map(local, mesh=mesh, in_specs=in_specs, out_specs=out_specs, check_vma=False)
```

time: 999 us -> 121 us (0.12)
  matrix products: 394 us -> 2.4 us
  other arithmetic: 232 us -> 3.53 us
  local copies, waits for them, and re-layouts: 225 us -> 7.65 us
  Pallas kernels: 0 us -> 51.9 us
  loops' own time: 48.2 us -> 0 us
  blocking collectives: 66.7 us -> 24.1 us
  waiting for transfers between devices: 1.17 us -> 13 us
  starting transfers between devices: 14.5 us -> 3.15 us
    dot_general x250 -> x4, matrix products: 394 us -> 2.4 us  [the longest x2 1.14 us: dotf(): return lax.dot_general(a, b, dims, preferred_element_type=F32)]
    scatter-add x50 -> x0, other arithmetic: 211 us -> none  [the longest x16 98.6 us: edge_block(): grad_pos = grad_pos.at[:, slot_flat].add(pair_grad.reshape(3, -1))]
    gather x34 -> x0, local copies, waits for them, and re-layouts: 97.5 us -> none  [the longest x16 51.3 us: edge_block(): table_feats[slot_flat]]
    psum x2 -> x0, blocking collectives: 66.7 us -> none  [the longest x1 33.9 us: local(): charge_sums = lax.psum(jnp.sum(charges_raw, 0), 'dom')]
    while x353 -> x0, local copies, waits for them, and re-layouts: 57.9 us -> none
    pallas_call x0 -> x2, Pallas kernels: none -> 51.9 us  [the longest x1 30.3 us: local(): pl.pallas_call(functools.partial(edge_kernel, slots), out_shape=(jax.Shap...]
    dynamic_slice x96 -> x0, local copies, waits for them, and re-layouts: 50.1 us -> none  [the longest x48 28.2 us: long_factors(): lax.scan(factor_block, None, jnp.arange(number_of_modes // kblock, dtype=...]
    another operation x3 -> x0, loops' own time: 48.2 us -> none  [the longest x1 18.6 us: long_backward(): lax.scan(force_block, initial, jnp.arange(real_grad.shape[1] // kblock, d...]
  transfers between devices with their start and end apart: 9 -> 5, of which waited for: 1 -> 4; matrix products, arithmetic and copies ran while one was open for 79% -> 2% of each run, Pallas kernels for 0% -> 25%
where the time goes in v1:
time: 121 us; the launch traced here: 120 us
  Pallas kernels  51.9 us (43%)
  blocking collectives  24.1 us (20%)
  between operations  14.3 us (12%)
  waiting for transfers between devices  13 us (11%)
  local copies, waits for them, and re-layouts  7.65 us (6%)
  other arithmetic  3.53 us (3%)
  starting transfers between devices  3.15 us (3%)
  matrix products  2.4 us (2%)
    pallas_call x1, Pallas kernels, local(): pl.pallas_call(functools.partial(edge_kernel, slots), out_shape=(jax.Shap...  30.3 us
    all_gather x1, blocking collectives, long_range(): data = lax.all_gather(mine, 'dom', axis=1, tiled=True)  24.1 us
    pallas_call x1, Pallas kernels, long_range(): pl.pallas_call(functools.partial(long_kernel, nk, 1.0 / side), out_shape=...  21.6 us
    unnamed x27, local copies, waits for them, and re-layouts  6.5 us
    ppermute x2, waiting for transfers between devices, shift_pair(): from_prev = lax.ppermute(to_next, 'dom', forward)  6.01 us
    reduce_scatter x1, waiting for transfers between devices, long_range(): mine = lax.psum_scatter(out, 'dom', scatter_dimension=1, tiled=True)  5.24 us
    ppermute x2, starting transfers between devices, shift_pair(): from_next = lax.ppermute(to_prev, 'dom', backward)  2.61 us
  transfers between devices with their start and end apart: 5, of which 4 were waited for; matrix products, arithmetic and copies ran while one was open for 2% of the time, Pallas kernels for 25%

profile of v1, /device:TPU:0, one launch (start us, length us, event | category | flops | bytes accessed | tf_op | source)
XLA Modules:
  0.0 120.1 jit_solution(7336353322876064476)
XLA Ops:
  7.2 0.0 reduce-scatter.2.cloned.1.call-start
  7.3 0.5 copy-done
  7.9 1.0 fusion.42
  8.8 0.1 pad.32.clone
  8.9 0.1 maximum_maximum_fusion
  9.0 24.1 %all_gather.3.data_ref = f32[24,4096]{1,0:T(8,128)S(1)} all-gather(f32[24,256]{1,0:T(8,128)S(1)} %maximum_maximum_fusion), channel_id=1, replica_groups=mesh['groups'=2,'dom'=16] {'dom'}, dimensions={1}, use_global_device_ids=true | all-gather | bytes 417792 | tf_op jit(solution)/shard_map/all_gather | solution.py:176
  33.1 0.1 slice_reduce_fusion.1
  33.3 0.1 copy.35.mean_ref
  33.4 0.1 copy.36.kp_ref
  33.5 0.1 copy.37.wave_ref
  33.6 0.1 fusion.23
  33.7 21.6 %long_range.1 = f32[24,4096]{1,0:T(8,128)S(1)} custom-call(f32[24,4096]{1,0:T(8,128)S(1)} %all_gather.3.data_ref, f32[16,1]{1,0:T(8,128)S(1)} %copy.35.mean_ref, f32[2,48,1]{2,1,0:T(8,128)S(1)} %copy.36.kp_ref, f32[2,48,1]{2,1,0:T(8,128)S(1)} %copy.37.wave_ref, f32[256,48]{1,0:T(8,128)S(1)} %bitcast.33), custom_call_target="tpu_custom_call" | custom-call | flops 4000000000 | bytes 2000000 | tf_op jit(solution)/shard_map/long_range/pallas_call | solution.py:200
  55.4 0.1 slice_reduce_fusion
  55.5 0.8 pad_maximum_fusion
  56.4 0.8 copy-done.4
  57.2 0.1 copy.26
  57.3 0.6 copy-done.9
  58.0 0.2 convolution_convert_fusion
  58.2 0.1 fusion.41
  58.3 0.5 collective-permute-start
  58.8 0.2 copy-done.5
  59.0 0.5 copy-done.7
  59.5 0.1 copy.25
  59.6 0.1 reshape.252.idx_ref
  59.8 0.1 reshape.251
  59.9 0.7 copy-done.3
  60.6 0.1 copy.28
  60.7 0.6 copy-done.1
  61.3 0.1 copy.29
  61.4 0.6 copy-done.2
  62.1 0.1 copy.30
  62.2 0.7 copy-done.8
  62.9 0.1 copy.32.eproj_ref
  63.0 1.5 %collective-permute-done = bf16[152,64]{1,0:T(8,128)(2,1)S(1)} collective-permute-done((bf16[152,64]{1,0:T(8,128)(2,1)S(1)}, bf16[152,64]{1,0:T(8,128)(2,1)S(1)}, u32[]{:S(2)}, u32[]{:S(2)}) %collective-permute-start) | collective-permute-done | bytes 19488 | tf_op jit(solution)/shard_map/ppermute | solution.py:234
  64.5 0.1 fusion.3.table_ref
  64.5 30.3 %edges.1 = (f32[144,384]{1,0:T(8,128)S(1)}, f32[8,16,32]{2,1,0:T(8,128)S(1)}) custom-call(s32[8,1,2048]{2,1,0:T(1,128)S(1)} %reshape.252.idx_ref, bf16[160,384]{1,0:T(8,128)(2,1)S(1)} %fusion.3.table_ref, bf16[8,24,32]{2,1,0:T(8,128)(2,1)S(1)} %bitcast.34, bf16[128,16]{1,0:T(8,128)(2,1)S(1)} %bitcast.35, bf16[16,128]{1,0:T(8,128)(2,1)S(1)} %copy-done.3, ...), custom_call_target="tpu_custom_call" | custom-call | flops 8000000000 | bytes 2000000 | tf_op jit(solution)/shard_map/edges/pallas_call | solution.py:273
  94.9 0.1 fusion.11
  95.0 2.6 %collective-permute-start.3 = (f32[136,64]{1,0:T(8,128)S(1)}, f32[136,64]{1,0:T(8,128)S(1)}, u32[]{:S(2)}, u32[]{:S(2)}) collective-permute-start(f32[136,64]{1,0:T(8,128)S(1)} %get-tuple-element.11), channel_id=1, source_target_pairs={{1,0},{2,1},{3,2},{4,3},{5,4},{6,5},{7,6},{8,7},{9,8},{10,9},{11,1... | collective-permute-start | bytes 104456 | tf_op jit(solution)/shard_map/ppermute | solution.py:235
  97.6 0.1 slice.75
  97.7 0.1 slice.73
  97.8 1.8 %collective-permute-done.3 = f32[136,64]{1,0:T(8,128)S(1)} collective-permute-done((f32[136,64]{1,0:T(8,128)S(1)}, f32[136,64]{1,0:T(8,128)S(1)}, u32[]{:S(2)}, u32[]{:S(2)}) %collective-permute-start.3) | collective-permute-done | bytes 34848 | tf_op jit(solution)/shard_map/ppermute | solution.py:235
  99.5 4.5 %collective-permute-done.2 = f32[136,64]{1,0:T(8,128)S(1)} collective-permute-done((f32[136,64]{1,0:T(8,128)S(1)}, f32[136,64]{1,0:T(8,128)S(1)}, u32[]{:S(2)}, u32[]{:S(2)}) %collective-permute-start.2) | collective-permute-done | bytes 34848 | tf_op jit(solution)/shard_map/ppermute | solution.py:234
  104.0 0.3 convolution_add_fusion
  104.3 5.2 %reduce-scatter.2.cloned.1.call-done = f32[24,256]{1,0:T(8,128)} async-done(((f32[24,4096]{1,0:T(8,128)}), f32[24,256]{1,0:T(8,128)}) %reduce-scatter.2.cloned.1.call-update) | async-done | bytes 24592 | tf_op jit(solution)/shard_map/reduce_scatter | solution.py:224
  109.6 0.7 fusion.37
  110.3 1.0 fusion.15
  111.3 0.7 copy.39
  112.0 1.3 %fusion.26 = f32[3,256]{1,0:T(4,128)} fusion(f32[24,256]{1,0:T(8,128)} %reduce-scatter.2.cloned.1.call-done, f32[3,256]{1,0:T(4,128)S(1)} %slice.75, f32[3,256]{1,0:T(4,128)S(1)} %slice.73, f32[136,256]{1,0:T(8,128)S(1)} %convolution_add_fusion), kind=kLoop, calls=%fused_computation.57 | loop fusion | flops 3072 | bytes 15360 | tf_op jit(solution)/shard_map/neg | solution.py:305
  (43 shorter events, 0.4 us)
Async XLA Ops:
  7.2 0.7 copy-start
  7.2 102.4 %reduce-scatter.2.cloned.1.call-start = ((), (), s32[]{:S(2)}) async-start(), calls=%async_computation.1 | async-start | bytes 417792 | tf_op jit(solution)/shard_map/reduce_scatter | solution.py:224
  7.9 1.1 copy-start.6
  56.3 0.8 copy-start.4
  57.3 0.7 copy-start.9
  58.2 0.8 copy-start.5
  58.3 4.7 %collective-permute-start.1 = (bf16[152,64]{1,0:T(8,128)(2,1)S(1)}, bf16[152,64]{1,0:T(8,128)(2,1)S(1)}, u32[]{:S(2)}, u32[]{:S(2)}) collective-permute-start(bf16[152,64]{1,0:T(8,128)(2,1)S(1)} %get-tuple-element.15), channel_id=1, source_target_pairs={{1,0},{2,1},{3,2},{4,3},{5,4},{6,5},{7,6},{8,7},{9,8},{10,9},{11,1... | collective-permute-start | bytes 58376 | tf_op jit(solution)/shard_map/ppermute | solution.py:235
  58.3 6.2 %collective-permute-start = (bf16[152,64]{1,0:T(8,128)(2,1)S(1)}, bf16[152,64]{1,0:T(8,128)(2,1)S(1)}, u32[]{:S(2)}, u32[]{:S(2)}) collective-permute-start(bf16[152,64]{1,0:T(8,128)(2,1)S(1)} %get-tuple-element.14), channel_id=1, source_target_pairs={{0,1},{1,2},{2,3},{3,4},{4,5},{5,6},{6,7},{7,8},{8,9},{9,10},{10,1... | collective-permute-start | bytes 58376 | tf_op jit(solution)/shard_map/ppermute | solution.py:234
  58.8 0.7 copy-start.7
  59.9 0.7 copy-start.3
  60.6 0.8 copy-start.1
  61.3 0.8 copy-start.2
  62.2 0.7 copy-start.8
  95.0 4.5 %collective-permute-start.3 = (f32[136,64]{1,0:T(8,128)S(1)}, f32[136,64]{1,0:T(8,128)S(1)}, u32[]{:S(2)}, u32[]{:S(2)}) collective-permute-start(f32[136,64]{1,0:T(8,128)S(1)} %get-tuple-element.11), channel_id=1, source_target_pairs={{1,0},{2,1},{3,2},{4,3},{5,4},{6,5},{7,6},{8,7},{9,8},{10,9},{11,1... | collective-permute-start | bytes 104456 | tf_op jit(solution)/shard_map/ppermute | solution.py:235
  97.6 6.5 %collective-permute-start.2 = (f32[136,64]{1,0:T(8,128)S(1)}, f32[136,64]{1,0:T(8,128)S(1)}, u32[]{:S(2)}, u32[]{:S(2)}) collective-permute-start(f32[136,64]{1,0:T(8,128)S(1)} %get-tuple-element.10), channel_id=1, source_target_pairs={{0,1},{1,2},{2,3},{3,4},{4,5},{5,6},{6,7},{7,8},{8,9},{9,10},{10,1... | collective-permute-start | bytes 104456 | tf_op jit(solution)/shard_map/ppermute | solution.py:234
Sparse Core Ops, SparseCore 0:
  56.5 53.0 reduce-scatter.1

commit v2 on v1

v2 whole, which is shorter than its diff:
```python
import functools
import math

import jax
import jax.numpy as jnp
from jax import lax
from jax.experimental import pallas as pl
from jax.experimental.pallas import tpu as pltpu
from jax.sharding import PartitionSpec as P

CELL_SIDE = 4.0
PREC_HIGH = lax.Precision.HIGHEST
F32 = jnp.float32
BF16 = jnp.bfloat16
NT = (((1,), (1,)), ((), ()))
NN = (((1,), (0,)), ((), ()))
TN = (((0,), (0,)), ((), ()))
MODES_X = 48
MODES_Y = 16
MODES_Z = 16


def dotf(a, b, dims=NN):
    return lax.dot_general(a, b, dims, preferred_element_type=F32)


def split2(a):
    hi = a.astype(BF16)
    return hi, (a - hi.astype(F32)).astype(BF16)


def split3(a):
    hi = lax.reduce_precision(a, 8, 7)
    mid = lax.reduce_precision(a - hi, 8, 7)
    return hi.astype(BF16), mid.astype(BF16), (a - hi - mid).astype(BF16)


def dot3(a, b, dims):
    ah, al = a
    bh, bl = b
    return dotf(ah, bh, dims) + (dotf(al, bh, dims) + dotf(ah, bl, dims))


def sincos_turns(turns):
    x = (turns - jnp.round(turns)) * (2.0 * math.pi)
    x2 = x * x
    c = jnp.full_like(x, 1.0 / math.factorial(16))
    for n in range(14, -1, -2):
        c = c * x2 + (-1.0) ** (n // 2) / math.factorial(n)
    s = jnp.full_like(x, 1.0 / math.factorial(17))
    for n in range(15, 0, -2):
        s = s * x2 + (-1.0) ** (n // 2) / math.factorial(n)
    return c, s * x


def edge_block(slots, idx, own_parts, table, weights, one, owner):
    w1t_ref, w1_ref, w2t_ref, w2_ref, w3t_ref, w3_ref, eproj_ref, decay_ref = weights
    scale = slots ** (-0.5)
    chan = w3t_ref.shape[0]
    got = dotf(table, one)
    feats = got[:chan]
    own = dotf(own_parts, owner)
    sep = got[chan : chan + 8] - own[0:8]
    for n in (8, 16):
        sep = sep + (got[chan + n : chan + n + 8] - own[n : n + 8])
    sep = sep + got[chan + 24 : chan + 32]
    sq = jnp.sum(sep * sep, 0, keepdims=True)
    decay = decay_ref[...]
    basis = jnp.exp(-decay * sq)
    pre1 = dotf(w1t_ref[...], basis.astype(BF16))
    sig1 = 0.5 * jnp.tanh(0.5 * pre1) + 0.5
    h1 = pre1 * sig1
    slope1 = sig1 + h1 * (1.0 - sig1)
    pre2 = dotf(w2t_ref[...], h1.astype(BF16))
    sig2 = 0.5 * jnp.tanh(0.5 * pre2) + 0.5
    h2 = pre2 * sig2
    slope2 = sig2 + h2 * (1.0 - sig2)
    filters = dotf(w3t_ref[...], h2.astype(BF16))
    prod_hi, prod_lo = split2(filters * feats)
    message = scale * (dotf(prod_hi, owner, NT) + dotf(prod_lo, owner, NT))
    sigm = 1.0 / (1.0 + jnp.exp(-message))
    out_slope = scale * eproj_ref[...] * (sigm * (1.0 + message * (1.0 - sigm)))
    os_hi, os_lo = split2(out_slope)
    slope_e = dotf(os_hi, owner) + dotf(os_lo, owner)
    fgrad = (slope_e * feats).astype(BF16)
    g2 = (dotf(w3_ref[...], fgrad) * slope2).astype(BF16)
    g1 = (dotf(w2_ref[...], g2) * slope1).astype(BF16)
    bg = dotf(w1_ref[...], g1)
    sgrad = -2.0 * jnp.sum(decay * basis * bg, 0, keepdims=True)
    pair_hi, pair_lo = split2(sgrad * sep)
    pairs = jnp.concatenate([pair_hi, pair_lo], 0)
    feat_part = dotf((filters * slope_e).astype(BF16), one, NT)
    pos_part = dotf(pairs, one, NT)
    own_part = dotf(pairs, owner, NT)
    return feat_part, pos_part[:8] + pos_part[8:], own_part[:8] + own_part[8:]


def layer_kernel(n, slots, inv_side, inv_total, sent_ref, mine_ref, data_ref, idx_ref, own_ref, pick_ref, proj_ref, kp_ref, wave_ref, wt_ref, w1t_ref, w1_ref, w2t_ref, w2_ref, w3t_ref, w3_ref, eproj_ref, decay_ref, feat_ref, pos_ref, own_out_ref, halo, table, gath, acc, ret_send, ret, sf, mh, ml, res_send, res, halo_ss, halo_rs, gath_ss, gath_rs, ret_ss, ret_rs, res_ss, res_rs):
    me = lax.axis_index("dom")
    after, before = lax.rem(me + 1, n), lax.rem(me + n - 1, n)
    mesh_id = pl.DeviceIdType.MESH

    def loop(first, last, body):
        def step(t, carry):
            body(t)
            return carry

        lax.fori_loop(first, last, step, 0)

    def remote(src, dst, ss, rs, target):
        return pltpu.make_async_remote_copy(
            src_ref=src, dst_ref=dst, send_sem=ss, recv_sem=rs, device_id={"dom": target}, device_id_type=mesh_id
        )

    barrier = pltpu.get_barrier_semaphore()
    loop(1, n, lambda t: pl.semaphore_signal(barrier, inc=1, device_id={"dom": lax.rem(me + t, n)}, device_id_type=mesh_id))
    pl.semaphore_wait(barrier, n - 1)

    def halo_copy(k):
        return remote(sent_ref.at[k], halo.at[k], halo_ss.at[k], halo_rs.at[k], (after, before)[k])

    def ret_copy(k):
        return remote(ret_send, ret.at[k], ret_ss.at[k], ret_rs.at[k], (before, after)[k])

    def gath_copy(t):
        return remote(data_ref, gath.at[t], gath_ss.at[t], gath_rs.at[t], lax.rem(me + t, n))

    def res_copy(t):
        return remote(res_send.at[t], res.at[t], res_ss.at[t], res_rs.at[t], lax.rem(me + n - t, n))

    halo_copy(0).start()
    halo_copy(1).start()
    loop(1, n, lambda t: gath_copy(t).start())
    gath[0] = data_ref[...]

    here = mine_ref.shape[1]
    edges = idx_ref.shape[2]
    atoms = own_ref.shape[2]
    rows = table.shape[1]
    wide = w3t_ref.shape[0]
    chan = proj_ref.shape[1]
    weights = (w1t_ref, w1_ref, w2t_ref, w2_ref, w3t_ref, w3_ref, eproj_ref, decay_ref)
    first = lax.broadcasted_iota(jnp.int32, (atoms, edges), 0) * slots
    edge_id = lax.broadcasted_iota(jnp.int32, (atoms, edges), 1)
    owner = jnp.where((edge_id >= first) & (edge_id < first + slots), 1.0, 0.0).astype(BF16)
    table[:, :here] = mine_ref[...]
    acc[...] = jnp.zeros_like(acc)
    halo_copy(0).wait()
    halo_copy(1).wait()
    table[:, here:] = halo[0] + halo[1]

    def edge_step(i):
        one = jnp.where(lax.broadcasted_iota(jnp.int32, (rows, edges), 0) == idx_ref[i], 1.0, 0.0).astype(BF16)
        feat_part, pos_part, own_part = edge_block(slots, idx_ref[i], own_ref[i], table[...], weights, one, owner)
        acc[0:wide, :] += feat_part
        acc[wide:, :] += pos_part
        own_out_ref[i] = own_part

    loop(0, idx_ref.shape[0], edge_step)
    ret_send[...] = acc[:, here:]
    ret_copy(0).start()
    ret_copy(1).start()

    loop(1, n, lambda t: gath_copy(t).wait())
    raw_sum = lax.fori_loop(0, n, lambda t, c: c + gath[t, 0:chan, :], jnp.zeros((chan, here), F32))
    mean = jnp.sum(raw_sum, 1, keepdims=True) * inv_total

    mp = kp_ref.shape[1]
    half = chan * MODES_Z
    k2 = lax.broadcasted_iota(jnp.int32, (MODES_Z, 1), 0).astype(F32) - float(MODES_Z // 2)

    def factors(t):
        q = gath[t, 0:chan, :] - mean
        xyz = gath[t, chan : chan + 8, :]
        x = xyz[0:1] * inv_side
        y = xyz[1:2] * (1.0 / CELL_SIDE)
        z = xyz[2:3] * (1.0 / CELL_SIDE)
        ec, es = sincos_turns(kp_ref[0] * x + kp_ref[1] * y)
        zc, zs = sincos_turns(k2 * z)
        a_re = (q[:, None, :] * zc[None, :, :]).reshape(half, here)
        a_im = (q[:, None, :] * zs[None, :, :]).reshape(half, here)
        return q, ec, es, zc, zs, [a_re, a_im]

    sf[...] = jnp.zeros_like(sf)

    def forward(t):
        q, ec, es, zc, zs, a = factors(t)
        sf[...] += dot3(split2(jnp.concatenate(a + [zc, zs], 0)), split2(jnp.concatenate([ec, es], 0)), NT)

    loop(0, n, forward)
    wt = wt_ref[...]
    re = wt * (sf[:half, :mp] - sf[half : 2 * half, mp:])
    im = wt * (sf[:half, mp:] + sf[half : 2 * half, :mp])
    m1 = 2 * half + MODES_Z
    one_re = sf[2 * half : m1, :mp] - sf[m1:, mp:]
    one_im = sf[2 * half : m1, mp:] + sf[m1:, :mp]
    both = re.reshape(chan, MODES_Z, mp) * one_re[None] + im.reshape(chan, MODES_Z, mp) * one_im[None]
    grad_mean = jnp.sum(jnp.sum(both, 1), 1, keepdims=True) * inv_total
    m = jnp.concatenate([jnp.concatenate([re, im], 1), jnp.concatenate([im, -re], 1)], 0)
    hi, lo = split2(m)
    mh[...] = hi
    ml[...] = lo

    def backward(t):
        q, ec, es, zc, zs, a = factors(t)
        mm = (mh[...], ml[...])
        u = dot3(mm, split2(jnp.concatenate([ec, es], 0)), NN)
        ur = u[:half].reshape(chan, MODES_Z, here)
        ui = u[half:].reshape(chan, MODES_Z, here)
        cg = jnp.sum(zc[None] * ur + zs[None] * ui, 1) - grad_mean
        kz = k2 * (2.0 * math.pi / CELL_SIDE)
        lz = jnp.sum((kz * zc)[None] * ui - (kz * zs)[None] * ur, 1)
        lz = jnp.sum(q * lz, 0, keepdims=True)
        p = dot3(mm, split2(jnp.concatenate(a, 0)), TN)
        dp = ec * p[mp:] - es * p[:mp]
        lx = jnp.sum(wave_ref[0] * dp, 0, keepdims=True)
        ly = jnp.sum(wave_ref[1] * dp, 0, keepdims=True)
        return jnp.concatenate([cg, lx, ly, lz, jnp.zeros((5, here), F32)], 0)

    def send_back(t):
        res_send[t] = backward(t)
        res_copy(t).start()

    loop(1, n, send_back)
    res[0] = backward(0)
    ret_copy(0).wait()
    ret_copy(1).wait()
    back_hi, back_lo = split2(jnp.concatenate([ret[0], ret[1]], 1))
    back = dotf(back_hi, pick_ref[...], NT) + dotf(back_lo, pick_ref[...], NT)
    grads = acc[:, :here] + back
    loop(1, n, lambda t: res_copy(t).wait())
    total = lax.fori_loop(0, n, lambda t, c: c + res[t], jnp.zeros(res.shape[1:], F32))
    raw_hi, raw_lo = split2(total[:chan])
    feat_ref[...] = grads[:wide] + (dotf(proj_ref[...], raw_hi) + dotf(proj_ref[...], raw_lo))
    pos_ref[...] = grads[wide:] + total[chan:]


def local(places, nodes, partners, counts, exported, modes, proj, w1, w2, w3, eproj):
    n = lax.axis_size("dom")
    me = lax.axis_index("dom")
    here, wide = nodes.shape
    halo = exported.shape[0] // 2
    slots = partners.shape[1]
    side = float(n)
    total = n * here
    nrbf = w1.shape[0]
    chan = proj.shape[1]
    nodes_t = nodes.T

    pad8 = lambda a: jnp.pad(a, ((0, 5), (0, 0)))
    parts = jnp.concatenate([pad8(a) for a in split3(places)], 0)
    mine = jnp.concatenate([nodes_t, parts, jnp.zeros((8, here), BF16)], 0)
    order = jnp.concatenate([exported[halo:], exported[:halo]])
    lane = jnp.arange(4 * halo, dtype=jnp.int32)
    keep = (lane < halo) | (lane >= 3 * halo)
    target = jnp.where(keep, jnp.concatenate([order, order]), -1)
    pick = (jnp.arange(here, dtype=jnp.int32)[:, None] == target[None, :]).astype(BF16)
    step = jnp.where((lane < halo) & (me == n - 1), -side, 0.0) + jnp.where((lane >= 3 * halo) & (me == 0), side, 0.0)
    row = jnp.arange(wide + 32, dtype=jnp.int32)[:, None]
    sent = (dotf(mine, pick) + jnp.where(row == wide + 24, step[None, :], 0.0)).astype(BF16)
    sent = jnp.stack([sent[:, : 2 * halo], sent[:, 2 * halo :]])

    data = jnp.concatenate([dotf(proj.T, nodes_t), places, jnp.zeros((5, here), F32)], 0)
    pairs = MODES_X * MODES_Y
    m = -(-pairs // n)
    mp = -(-m // 8) * 8
    local_p = jnp.arange(mp, dtype=jnp.int32)
    flat = me * m + local_p
    real = (local_p < m) & (flat < pairs)
    k0 = (flat // MODES_Y + 1).astype(F32)
    k1 = (flat % MODES_Y - MODES_Y // 2).astype(F32)
    kx, ky = k0 * (2.0 * math.pi / side), k1 * (2.0 * math.pi / CELL_SIDE)
    kz = (jnp.arange(MODES_Z) - MODES_Z // 2).astype(F32) * (2.0 * math.pi / CELL_SIDE)
    ksq = (kx * kx + ky * ky)[None, :] + (kz * kz)[:, None]
    coupling = float(total * modes.shape[1]) ** (-0.5)
    wt = 2.0 * coupling * 4.0 * jnp.exp(-ksq / 1024.0) / (ksq + 0.25)
    wt = jnp.tile(jnp.where(real[None, :], wt, 0.0), (chan, 1))
    kp = jnp.stack([k0, k1])[:, :, None]
    wave = jnp.stack([kx, ky])[:, :, None]
    half = chan * MODES_Z

    blk = math.gcd(here, 32)
    nblk = here // blk
    edges = blk * slots
    live = jnp.arange(slots, dtype=jnp.int32)[None, :] < counts[:, None]
    idx = jnp.where(live, partners, -1).reshape(nblk, 1, edges)
    own = parts.reshape(24, nblk, blk).transpose(1, 0, 2)
    decay = (0.02 * 64.0 ** (jnp.arange(nrbf, dtype=F32) / (nrbf - 1)))[:, None]
    args = [sent, mine, data, idx, own, pick, proj, kp, wave, wt]
    args += [w1.T, w1, w2.T, w2, w3.T, w3, eproj[:, None], decay]
    vmem = pl.BlockSpec(memory_space=pltpu.VMEM)
    dma = pltpu.SemaphoreType.DMA
    borrowed = 2 * halo
    feat, pos, own_out = pl.pallas_call(
        functools.partial(layer_kernel, n, slots, 1.0 / side, 1.0 / total),
        out_shape=(
            jax.ShapeDtypeStruct((wide, here), F32),
            jax.ShapeDtypeStruct((8, here), F32),
            jax.ShapeDtypeStruct((nblk, 8, blk), F32),
        ),
        in_specs=[vmem] * len(args),
        out_specs=(vmem,) * 3,
        scratch_shapes=[
            pltpu.VMEM((2, wide + 32, borrowed), BF16),
            pltpu.VMEM((wide + 32, here + borrowed), BF16),
            pltpu.VMEM((n, chan + 8, here), F32),
            pltpu.VMEM((wide + 8, here + borrowed), F32),
            pltpu.VMEM((wide + 8, borrowed), F32),
            pltpu.VMEM((2, wide + 8, borrowed), F32),
            pltpu.VMEM((2 * half + 2 * MODES_Z, 2 * mp), F32),
            pltpu.VMEM((2 * half, 2 * mp), BF16),
            pltpu.VMEM((2 * half, 2 * mp), BF16),
            pltpu.VMEM((n, chan + 8, here), F32),
            pltpu.VMEM((n, chan + 8, here), F32),
            dma((2,)), dma((2,)), dma((n,)), dma((n,)), dma((2,)), dma((2,)), dma((n,)), dma((n,)),
        ],
        compiler_params=pltpu.CompilerParams(collective_id=0, has_side_effects=True, vmem_limit_bytes=56 * 2**20),
        name="layer",
    )(*args)
    own_sum = own_out.transpose(1, 0, 2).reshape(8, here)
    forces = own_sum[:3] - pos[:3]
    return (forces, feat.T.astype(BF16))


def solution(mesh):
    both = ("groups", "dom")
    in_specs = (P(None, both), P(both, None), P(both, None), P(both), P(both)) + (P(),) * 6
    out_specs = (P(None, both), P(both, None))
    return jax.shard_map(local, mesh=mesh, in_specs=in_specs, out_specs=out_specs, check_vma=False)
```

time: 121 us -> 85.2 us (0.70)
  blocking collectives: 24.1 us -> 0 us
  Pallas kernels: 51.9 us -> 66.2 us
  between operations: 14.3 us -> 0.79 us
  waiting for transfers between devices: 13 us -> 0 us
  local copies, waits for them, and re-layouts: 7.65 us -> 11.6 us
  starting transfers between devices: 3.15 us -> 0 us
  other arithmetic: 3.53 us -> 5.73 us
  matrix products: 2.4 us -> 0.31 us
    all_gather x1 -> x0, blocking collectives: 24.1 us -> none  [long_range(): data = lax.all_gather(mine, 'dom', axis=1, tiled=True)]
    pallas_call x2 -> x1, Pallas kernels: 51.9 us -> 66.2 us  [local(): pl.pallas_call(functools.partial(layer_kernel, n, slots, 1.0 / side, 1.0...]
    ppermute x4 -> x0, waiting for transfers between devices: 7.77 us -> none  [the longest x2 6.01 us: shift_pair(): from_prev = lax.ppermute(to_next, 'dom', forward)]
    reduce_scatter x1 -> x0, waiting for transfers between devices: 5.24 us -> none  [long_range(): mine = lax.psum_scatter(out, 'dom', scatter_dimension=1, tiled=True)]
    ppermute x4 -> x0, starting transfers between devices: 3.11 us -> none  [the longest x2 2.61 us: shift_pair(): from_next = lax.ppermute(to_prev, 'dom', backward)]
    broadcast_in_dim x4, local copies, waits for them, and re-layouts: 0.31 us -> 2.19 us  [the longest x1 0.73 us: local(): kp = jnp.stack([k0, k1])[:, :, None]]
    convert_element_type x2 -> x3, other arithmetic: 0.03 us -> 1.61 us  [the longest x1 0.91 us: local(): return (forces, feat.T.astype(BF16))]
    slice x8 -> x4, local copies, waits for them, and re-layouts: 0.3 us -> 1.65 us  [the longest x3 0.85 us: local(): forces = own_sum[:3] - pos[:3]]
  transfers between devices with their start and end apart: 5 -> 0, of which waited for: 4 -> 0; matrix products, arithmetic and copies ran while one was open for 2% -> 0% of each run, Pallas kernels for 25% -> 0%
where the time goes in v2:
time: 85.2 us; the launch traced here: 84.6 us
  Pallas kernels  66.2 us (78%)
  local copies, waits for them, and re-layouts  11.6 us (14%)
  other arithmetic  5.73 us (7%)
    pallas_call x1, Pallas kernels, local(): pl.pallas_call(functools.partial(layer_kernel, n, slots, 1.0 / side, 1.0...  66.2 us
    unnamed x29, local copies, waits for them, and re-layouts  5.46 us

profile of v2, /device:TPU:0, one launch (start us, length us, event | category | flops | bytes accessed | tf_op | source)
XLA Modules:
  0.0 84.6 jit_solution(8683299922275958168)
XLA Ops:
  0.6 0.0 copy-start.1
  0.7 0.1 pad.22.clone
  0.8 0.8 fusion.21
  1.6 0.7 or_select_fusion
  2.4 0.7 fusion.9
  3.1 0.1 fusion.8
  3.2 0.0 copy-start.7
  3.2 0.6 power_multiply_fusion.decay_ref
  3.8 0.0 copy-done.1
  3.8 0.1 copy-done.7
  3.9 0.0 copy-start.6
  3.9 0.1 fusion.22
  4.0 0.6 copy-done.6
  4.5 0.7 maximum_maximum_fusion.data_ref
  5.2 0.0 copy-start.5
  5.2 0.0 copy-start.2
  5.2 0.7 copy.29.proj_ref
  6.0 0.0 copy-done.5
  6.0 0.7 copy.25
  6.7 0.0 copy-done.2
  6.7 0.0 copy-start.3
  6.7 0.7 copy.26
  7.4 0.0 copy-done.3
  7.4 0.7 copy.27
  8.2 0.7 copy.31.wave_ref
  8.9 0.7 copy.30.kp_ref
  9.6 0.0 copy-done.4
  9.6 0.0 copy-done.9
  9.6 0.1 copy.23
  9.7 0.0 copy-start.10
  9.7 0.8 reshape.230.idx_ref
  10.5 0.0 copy-done.10
  10.5 0.7 copy.32.eproj_ref
  11.2 0.1 copy.22
  11.4 0.1 reshape.229
  11.5 0.6 copy.36
  12.1 0.2 fusion
  12.3 0.4 copy-done
  12.8 0.6 pad_maximum_fusion.sent_ref
  13.4 0.7 tile.4
  14.1 0.7 fusion.1.pick_ref
  14.8 66.2 %layer.1 = (f32[128,256]{1,0:T(8,128)}, f32[8,256]{1,0:T(8,128)}, f32[8,8,32]{2,1,0:T(8,128)}) custom-call(bf16[2,160,128]{2,1,0:T(8,128)(2,1)} %pad_maximum_fusion.sent_ref, bf16[160,256]{1,0:T(8,128)(2,1)} %copy-done, f32[24,256]{1,0:T(8,128)} %maximum_maximum_fusion.data_ref, s32[8,1,2048]{2,1,0:T(1,128)} %reshape.230.idx_ref, ...), custom_call_target="tpu_custom_call" | custom-call | tf_op jit(solution)/shard_map/layer/pallas_call | solution.py:294
  80.9 0.8 slice.31
  81.7 0.1 slice.27
  81.8 0.6 copy-done.8
  82.4 0.6 slice_subtract_fusion
  83.0 0.9 %convert_bitcast_fusion = bf16[256,128]{0,1:T(8,128)(2,1)S(1)} fusion(f32[128,256]{1,0:T(8,128)} %get-tuple-element.7), kind=kLoop, calls=%fused_computation.7 | loop fusion | flops 32768 | bytes 196608 | tf_op jit(solution)/shard_map/convert_element_type | solution.py:322
  83.9 0.7 copy.34
  (23 shorter events, 0.2 us)
Async XLA Ops:
  0.6 3.2 %copy-start.1 = (bf16[256,128]{1,0:T(8,128)(2,1)S(1)}, bf16[256,128]{1,0:T(8,128)(2,1)}, u32[]{:S(2)}) copy-start(bf16[256,128]{1,0:T(8,128)(2,1)} %param.12) | copy-start | bytes 196612
  3.2 0.7 copy-start.7
  3.9 0.7 copy-start.6
  5.2 0.7 copy-start.5
  5.2 1.4 %copy-start.2 = (bf16[128,128]{1,0:T(8,128)(2,1)S(1)}, bf16[128,128]{1,0:T(8,128)(2,1)}, u32[]{:S(2)}) copy-start(bf16[128,128]{1,0:T(8,128)(2,1)} %w2_ref.1) | copy-start | bytes 98308
  6.7 0.8 copy-start.3
  8.2 1.5 %copy-start.4 = (s32[256,64]{0,1:T(8,128)S(1)}, s32[256,64]{0,1:T(8,128)}, u32[]{:S(2)}) copy-start(s32[256,64]{0,1:T(8,128)} %param.13) | copy-start | bytes 196612
  8.9 0.7 copy-start.9
  9.7 0.8 copy-start.10
  12.1 0.6 copy-start
  81.7 0.7 copy-start.8

commit v3 on v2

--- a/solution.py
+++ b/solution.py
@@ -35,10 +35,8 @@
     return hi.astype(BF16), mid.astype(BF16), (a - hi - mid).astype(BF16)
 
 
-def dot3(a, b, dims):
-    ah, al = a
-    bh, bl = b
-    return dotf(ah, bh, dims) + (dotf(al, bh, dims) + dotf(ah, bl, dims))
+def dotb(a, b, dims):
+    return dotf(a.astype(BF16), b.astype(BF16), dims)
 
 
 def sincos_turns(turns):
@@ -95,7 +93,7 @@
     return feat_part, pos_part[:8] + pos_part[8:], own_part[:8] + own_part[8:]
 
 
-def layer_kernel(n, slots, inv_side, inv_total, sent_ref, mine_ref, data_ref, idx_ref, own_ref, pick_ref, proj_ref, kp_ref, wave_ref, wt_ref, w1t_ref, w1_ref, w2t_ref, w2_ref, w3t_ref, w3_ref, eproj_ref, decay_ref, feat_ref, pos_ref, own_out_ref, halo, table, gath, acc, ret_send, ret, sf, mh, ml, res_send, res, halo_ss, halo_rs, gath_ss, gath_rs, ret_ss, ret_rs, res_ss, res_rs):
+def layer_kernel(n, slots, m_here, coupling, inv_side, inv_total, sent_ref, mine_ref, data_ref, idx_ref, own_ref, pick_ref, proj_ref, w1_ref, w2_ref, w3_ref, eproj_ref, decay_ref, feat_ref, pos_ref, own_out_ref, w1t_ref, w2t_ref, w3t_ref, halo, table, gath, acc, ret_send, ret, sf, mh, res_send, res, halo_ss, halo_rs, gath_ss, gath_rs, ret_ss, ret_rs, res_ss, res_rs):
     me = lax.axis_index("dom")
     after, before = lax.rem(me + 1, n), lax.rem(me + n - 1, n)
     mesh_id = pl.DeviceIdType.MESH
@@ -145,6 +143,9 @@
     owner = jnp.where((edge_id >= first) & (edge_id < first + slots), 1.0, 0.0).astype(BF16)
     table[:, :here] = mine_ref[...]
     acc[...] = jnp.zeros_like(acc)
+    w1t_ref[...] = w1_ref[...].astype(F32).T.astype(BF16)
+    w2t_ref[...] = w2_ref[...].astype(F32).T.astype(BF16)
+    w3t_ref[...] = w3_ref[...].astype(F32).T.astype(BF16)
     halo_copy(0).wait()
     halo_copy(1).wait()
     table[:, here:] = halo[0] + halo[1]
@@ -165,8 +166,21 @@
     raw_sum = lax.fori_loop(0, n, lambda t, c: c + gath[t, 0:chan, :], jnp.zeros((chan, here), F32))
     mean = jnp.sum(raw_sum, 1, keepdims=True) * inv_total
 
-    mp = kp_ref.shape[1]
+    mp = mh.shape[1] // 2
     half = chan * MODES_Z
+
+    def pair_numbers(shape, dim):
+        local_p = lax.broadcasted_iota(jnp.int32, shape, dim)
+        flat = me * m_here + local_p
+        real = (local_p < m_here) & (flat < MODES_X * MODES_Y)
+        return (flat // MODES_Y + 1).astype(F32), (flat % MODES_Y - MODES_Y // 2).astype(F32), real
+
+    unit_x, unit_y = 2.0 * math.pi * inv_side, 2.0 * math.pi / CELL_SIDE
+    k0, k1, _ = pair_numbers((mp, 1), 0)
+    row0, row1, real = pair_numbers((half, mp), 1)
+    row2 = (lax.broadcasted_iota(jnp.int32, (half, mp), 0) % MODES_Z - MODES_Z // 2).astype(F32)
+    ksq = (row0 * unit_x) ** 2 + (row1 * unit_y) ** 2 + (row2 * unit_y) ** 2
+    wt = jnp.where(real, 8.0 * coupling * jnp.exp(-ksq / 1024.0) / (ksq + 0.25), 0.0)
     k2 = lax.broadcasted_iota(jnp.int32, (MODES_Z, 1), 0).astype(F32) - float(MODES_Z // 2)
 
     def factors(t):
@@ -175,7 +189,7 @@
         x = xyz[0:1] * inv_side
         y = xyz[1:2] * (1.0 / CELL_SIDE)
         z = xyz[2:3] * (1.0 / CELL_SIDE)
-        ec, es = sincos_turns(kp_ref[0] * x + kp_ref[1] * y)
+        ec, es = sincos_turns(k0 * x + k1 * y)
         zc, zs = sincos_turns(k2 * z)
         a_re = (q[:, None, :] * zc[None, :, :]).reshape(half, here)
         a_im = (q[:, None, :] * zs[None, :, :]).reshape(half, here)
@@ -185,10 +199,9 @@
 
     def forward(t):
         q, ec, es, zc, zs, a = factors(t)
-        sf[...] += dot3(split2(jnp.concatenate(a + [zc, zs], 0)), split2(jnp.concatenate([ec, es], 0)), NT)
+        sf[...] += dotb(jnp.concatenate(a + [zc, zs], 0), jnp.concatenate([ec, es], 0), NT)
 
     loop(0, n, forward)
-    wt = wt_ref[...]
     re = wt * (sf[:half, :mp] - sf[half : 2 * half, mp:])
     im = wt * (sf[:half, mp:] + sf[half : 2 * half, :mp])
     m1 = 2 * half + MODES_Z
@@ -197,24 +210,22 @@
     both = re.reshape(chan, MODES_Z, mp) * one_re[None] + im.reshape(chan, MODES_Z, mp) * one_im[None]
     grad_mean = jnp.sum(jnp.sum(both, 1), 1, keepdims=True) * inv_total
     m = jnp.concatenate([jnp.concatenate([re, im], 1), jnp.concatenate([im, -re], 1)], 0)
-    hi, lo = split2(m)
-    mh[...] = hi
-    ml[...] = lo
+    mh[...] = m.astype(BF16)
 
     def backward(t):
         q, ec, es, zc, zs, a = factors(t)
-        mm = (mh[...], ml[...])
-        u = dot3(mm, split2(jnp.concatenate([ec, es], 0)), NN)
+        mm = mh[...]
+        u = dotb(mm, jnp.concatenate([ec, es], 0), NN)
         ur = u[:half].reshape(chan, MODES_Z, here)
         ui = u[half:].reshape(chan, MODES_Z, here)
         cg = jnp.sum(zc[None] * ur + zs[None] * ui, 1) - grad_mean
         kz = k2 * (2.0 * math.pi / CELL_SIDE)
         lz = jnp.sum((kz * zc)[None] * ui - (kz * zs)[None] * ur, 1)
         lz = jnp.sum(q * lz, 0, keepdims=True)
-        p = dot3(mm, split2(jnp.concatenate(a, 0)), TN)
+        p = dotb(mm, jnp.concatenate(a, 0), TN)
         dp = ec * p[mp:] - es * p[:mp]
-        lx = jnp.sum(wave_ref[0] * dp, 0, keepdims=True)
-        ly = jnp.sum(wave_ref[1] * dp, 0, keepdims=True)
+        lx = jnp.sum((k0 * unit_x) * dp, 0, keepdims=True)
+        ly = jnp.sum((k1 * unit_y) * dp, 0, keepdims=True)
         return jnp.concatenate([cg, lx, ly, lz, jnp.zeros((5, here), F32)], 0)
 
     def send_back(t):
@@ -231,8 +242,10 @@
     loop(1, n, lambda t: res_copy(t).wait())
     total = lax.fori_loop(0, n, lambda t, c: c + res[t], jnp.zeros(res.shape[1:], F32))
     raw_hi, raw_lo = split2(total[:chan])
-    feat_ref[...] = grads[:wide] + (dotf(proj_ref[...], raw_hi) + dotf(proj_ref[...], raw_lo))
-    pos_ref[...] = grads[wide:] + total[chan:]
+    feat = grads[:wide] + (dotf(proj_ref[...], raw_hi) + dotf(proj_ref[...], raw_lo))
+    feat_ref[...] = feat.T.astype(BF16)
+    own_sum = jnp.concatenate([own_out_ref[i] for i in range(idx_ref.shape[0])], 1)
+    pos_ref[...] = (own_sum - (grads[wide:] + total[chan:]))[:3]
 
 
 def local(places, nodes, partners, counts, exported, modes, proj, w1, w2, w3, eproj):
@@ -264,19 +277,7 @@
     pairs = MODES_X * MODES_Y
     m = -(-pairs // n)
     mp = -(-m // 8) * 8
-    local_p = jnp.arange(mp, dtype=jnp.int32)
-    flat = me * m + local_p
-    real = (local_p < m) & (flat < pairs)
-    k0 = (flat // MODES_Y + 1).astype(F32)
-    k1 = (flat % MODES_Y - MODES_Y // 2).astype(F32)
-    kx, ky = k0 * (2.0 * math.pi / side), k1 * (2.0 * math.pi / CELL_SIDE)
-    kz = (jnp.arange(MODES_Z) - MODES_Z // 2).astype(F32) * (2.0 * math.pi / CELL_SIDE)
-    ksq = (kx * kx + ky * ky)[None, :] + (kz * kz)[:, None]
     coupling = float(total * modes.shape[1]) ** (-0.5)
-    wt = 2.0 * coupling * 4.0 * jnp.exp(-ksq / 1024.0) / (ksq + 0.25)
-    wt = jnp.tile(jnp.where(real[None, :], wt, 0.0), (chan, 1))
-    kp = jnp.stack([k0, k1])[:, :, None]
-    wave = jnp.stack([kx, ky])[:, :, None]
     half = chan * MODES_Z
 
     blk = math.gcd(here, 32)
@@ -286,21 +287,24 @@
     idx = jnp.where(live, partners, -1).reshape(nblk, 1, edges)
     own = parts.reshape(24, nblk, blk).transpose(1, 0, 2)
     decay = (0.02 * 64.0 ** (jnp.arange(nrbf, dtype=F32) / (nrbf - 1)))[:, None]
-    args = [sent, mine, data, idx, own, pick, proj, kp, wave, wt]
-    args += [w1.T, w1, w2.T, w2, w3.T, w3, eproj[:, None], decay]
+    args = [sent, mine, data, idx, own, pick, proj]
+    args += [w1, w2, w3, eproj[:, None], decay]
     vmem = pl.BlockSpec(memory_space=pltpu.VMEM)
     dma = pltpu.SemaphoreType.DMA
     borrowed = 2 * halo
-    feat, pos, own_out = pl.pallas_call(
-        functools.partial(layer_kernel, n, slots, 1.0 / side, 1.0 / total),
+    feature_grad, forces = pl.pallas_call(
+        functools.partial(layer_kernel, n, slots, m, coupling, 1.0 / side, 1.0 / total),
         out_shape=(
-            jax.ShapeDtypeStruct((wide, here), F32),
-            jax.ShapeDtypeStruct((8, here), F32),
-            jax.ShapeDtypeStruct((nblk, 8, blk), F32),
+            jax.ShapeDtypeStruct((here, wide), BF16),
+            jax.ShapeDtypeStruct((3, here), F32),
         ),
         in_specs=[vmem] * len(args),
-        out_specs=(vmem,) * 3,
+        out_specs=(vmem,) * 2,
         scratch_shapes=[
+            pltpu.VMEM((nblk, 8, blk), F32),
+            pltpu.VMEM((w1.shape[1], nrbf), BF16),
+            pltpu.VMEM(w2.shape, BF16),
+            pltpu.VMEM(w3.shape, BF16),
             pltpu.VMEM((2, wide + 32, borrowed), BF16),
             pltpu.VMEM((wide + 32, here + borrowed), BF16),
             pltpu.VMEM((n, chan + 8, here), F32),
@@ -309,7 +313,6 @@
             pltpu.VMEM((2, wide + 8, borrowed), F32),
             pltpu.VMEM((2 * half + 2 * MODES_Z, 2 * mp), F32),
             pltpu.VMEM((2 * half, 2 * mp), BF16),
-            pltpu.VMEM((2 * half, 2 * mp), BF16),
             pltpu.VMEM((n, chan + 8, here), F32),
             pltpu.VMEM((n, chan + 8, here), F32),
             dma((2,)), dma((2,)), dma((n,)), dma((n,)), dma((2,)), dma((2,)), dma((n,)), dma((n,)),
@@ -317,9 +320,7 @@
         compiler_params=pltpu.CompilerParams(collective_id=0, has_side_effects=True, vmem_limit_bytes=56 * 2**20),
         name="layer",
     )(*args)
-    own_sum = own_out.transpose(1, 0, 2).reshape(8, here)
-    forces = own_sum[:3] - pos[:3]
-    return (forces, feat.T.astype(BF16))
+    return (forces, feature_grad)
 
 
 def solution(mesh):

time: 85.2 us -> 72.1 us (0.85)
  Pallas kernels: 66.2 us -> 59.2 us
  local copies, waits for them, and re-layouts: 11.6 us -> 7.85 us
  other arithmetic: 5.73 us -> 2.72 us
  matrix products: 0.31 us -> 1.19 us
    pallas_call x1, Pallas kernels: 66.2 us -> 59.2 us  [local(): pl.pallas_call(functools.partial(layer_kernel, n, slots, m, coupling, 1.0...]
    broadcast_in_dim x3 -> x1, local copies, waits for them, and re-layouts: 2.19 us -> 0.75 us  [local(): args += [w1, w2, w3, eproj[:, None], decay]]
    convert_element_type x2 -> x0, other arithmetic: 0.93 us -> none  [the longest x1 0.91 us: local(): return (forces, feat.T.astype(BF16))]
    dot_general x2, matrix products: 0.31 us -> 1.19 us  [dotf(): return lax.dot_general(a, b, dims, preferred_element_type=F32)]
    unnamed x29 -> x21, local copies, waits for them, and re-layouts: 5.46 us -> 5.35 us
where the time goes in v3:
time: 72.1 us; the launch traced here: 71.7 us
  Pallas kernels  59.2 us (82%)
  local copies, waits for them, and re-layouts  7.85 us (11%)
  other arithmetic  2.72 us (4%)
  matrix products  1.19 us (2%)
  between operations  0.74 us (1%)
    pallas_call x1, Pallas kernels, local(): pl.pallas_call(functools.partial(layer_kernel, n, slots, m, coupling, 1.0...  59.2 us
    unnamed x21, local copies, waits for them, and re-layouts  5.35 us

profile of v3, /device:TPU:0, one launch (start us, length us, event | category | flops | bytes accessed | tf_op | source)
XLA Modules:
  0.0 71.7 jit_solution(13853192705168526539)
XLA Ops:
  0.7 0.1 pad.18.clone
  0.7 0.0 copy-start.5
  0.7 0.6 copy-done.5
  1.4 0.0 copy-start.3
  1.4 0.1 fusion.9
  1.5 0.1 or_select_fusion
  1.5 0.5 copy-done.3
  2.1 0.0 copy-start.4
  2.1 0.6 power_multiply_fusion.decay_ref
  2.7 0.1 copy-done.4
  2.8 0.0 copy-start.2
  2.8 1.0 %fusion.10 = f32[16,256]{1,0:T(8,128)S(1)} fusion(bf16[128,16]{0,1:T(8,128)(2,1)S(1)} %copy-done.4, bf16[256,128]{1,0:T(8,128)(2,1)} %param.12), kind=kOutput, calls=%fused_computation.35 | convolution fusion | flops 1048576 | bytes 86016 | tf_op jit(solution)/shard_map/dot_general | solution.py:24
  3.8 0.7 maximum_maximum_fusion.data_ref
  4.5 0.0 copy-start.6
  4.5 0.7 copy.20.proj_ref
  5.2 0.0 copy-done.2
  5.2 0.0 copy-done.6
  5.2 0.1 copy.17
  5.3 0.0 copy-start.7
  5.3 0.8 %reshape.67.idx_ref = s32[8,1,2048]{2,1,0:T(1,128)} reshape(s32[256,64]{1,0:T(8,128)S(1)} %copy.17) | data formatting | bytes 131072 | tf_op jit(solution)/shard_map/reshape | solution.py:287
  6.1 0.0 copy-done.7
  6.1 0.0 copy-start.1
  6.1 0.7 %copy.21.eproj_ref = f32[128,1]{1,0:T(8,128)} copy(f32[128,1]{0,1:T(1,128)S(1)} %bitcast.14) | data formatting | bytes 1024 | tf_op jit(solution)/shard_map/broadcast_in_dim | solution.py:291
  6.8 0.1 copy-done.1
  6.9 0.1 copy.16
  7.1 0.1 reshape.66
  7.2 0.6 copy.23
  7.8 0.0 copy-start
  7.8 0.2 fusion
  8.0 0.4 copy-done
  8.4 0.6 pad_maximum_fusion.sent_ref
  9.1 0.7 fusion.1.pick_ref
  9.7 59.2 %layer.1 = (bf16[256,128]{1,0:T(8,128)(2,1)}, f32[3,256]{1,0:T(4,128)}) custom-call(bf16[2,160,128]{2,1,0:T(8,128)(2,1)} %pad_maximum_fusion.sent_ref, bf16[160,256]{1,0:T(8,128)(2,1)} %copy-done, f32[24,256]{1,0:T(8,128)} %maximum_maximum_fusion.data_ref, s32[8,1,2048]{2,1,0:T(1,128)} %reshape.67.idx_ref, bf16[8,24,32]{2,1,0:T(8,128)(2,1)} %bitcast.13, ...), custom_call_target="tpu_custom_call" | custom-call | tf_op jit(solution)/shard_map/layer/pallas_call | solution.py:295
  69.0 1.3 %copy.30 = f32[3,256]{1,0:T(4,128)} copy(f32[3,256]{1,0:T(4,128)} %get-tuple-element.21) | data formatting | bytes 6144
  70.2 1.5 %copy.31 = bf16[256,128]{1,0:T(8,128)(2,1)} copy(bf16[256,128]{1,0:T(8,128)(2,1)} %get-tuple-element.22) | data formatting | bytes 131072
  (12 shorter events, 0.1 us)
Async XLA Ops:
  0.7 0.7 copy-start.5
  1.4 0.7 copy-start.3
  2.1 0.7 copy-start.4
  2.8 2.4 %copy-start.2 = (s32[256,64]{0,1:T(8,128)S(1)}, s32[256,64]{0,1:T(8,128)}, u32[]{:S(2)}) copy-start(s32[256,64]{0,1:T(8,128)} %param.13) | copy-start | bytes 196612
  4.5 0.7 copy-start.6
  5.3 0.8 %copy-start.7 = (f32[128]{0:T(128)S(1)}, f32[128]{0:T(128)}, u32[]{:S(2)}) copy-start(f32[128]{0:T(128)} %param.20) | copy-start | bytes 1540
  6.1 0.8 %copy-start.1 = (bf16[256,128]{1,0:T(8,128)(2,1)S(1)}, bf16[256,128]{1,0:T(8,128)(2,1)}, u32[]{:S(2)}) copy-start(bf16[256,128]{1,0:T(8,128)(2,1)} %param.12) | copy-start | bytes 196612
  7.8 0.6 copy-start

commit v4 on v3

--- a/solution.py
+++ b/solution.py
@@ -68,21 +68,22 @@
     pre1 = dotf(w1t_ref[...], basis.astype(BF16))
     sig1 = 0.5 * jnp.tanh(0.5 * pre1) + 0.5
     h1 = pre1 * sig1
-    slope1 = sig1 + h1 * (1.0 - sig1)
-    pre2 = dotf(w2t_ref[...], h1.astype(BF16))
+    h1b, sig1b = h1.astype(BF16), sig1.astype(BF16)
+    slope1 = sig1b + h1b * (1.0 - sig1b)
+    pre2 = dotf(w2t_ref[...], h1b)
     sig2 = 0.5 * jnp.tanh(0.5 * pre2) + 0.5
     h2 = pre2 * sig2
-    slope2 = sig2 + h2 * (1.0 - sig2)
-    filters = dotf(w3t_ref[...], h2.astype(BF16))
-    prod_hi, prod_lo = split2(filters * feats)
-    message = scale * (dotf(prod_hi, owner, NT) + dotf(prod_lo, owner, NT))
+    h2b, sig2b = h2.astype(BF16), sig2.astype(BF16)
+    slope2 = sig2b + h2b * (1.0 - sig2b)
+    filters = dotf(w3t_ref[...], h2b)
+    message = scale * dotf((filters * feats).astype(BF16), owner, NT)
     sigm = 1.0 / (1.0 + jnp.exp(-message))
     out_slope = scale * eproj_ref[...] * (sigm * (1.0 + message * (1.0 - sigm)))
     os_hi, os_lo = split2(out_slope)
-    slope_e = dotf(os_hi, owner) + dotf(os_lo, owner)
+    slope_e = dotf(jnp.concatenate([os_hi, os_lo], 1), jnp.concatenate([owner, owner], 0))
     fgrad = (slope_e * feats).astype(BF16)
-    g2 = (dotf(w3_ref[...], fgrad) * slope2).astype(BF16)
-    g1 = (dotf(w2_ref[...], g2) * slope1).astype(BF16)
+    g2 = dotf(w3_ref[...], fgrad).astype(BF16) * slope2
+    g1 = dotf(w2_ref[...], g2).astype(BF16) * slope1
     bg = dotf(w1_ref[...], g1)
     sgrad = -2.0 * jnp.sum(decay * basis * bg, 0, keepdims=True)
     pair_hi, pair_lo = split2(sgrad * sep)

time: 72.1 us -> 68.8 us (0.954)
  Pallas kernels: 59.2 us -> 55.9 us
    pallas_call x1, Pallas kernels: 59.2 us -> 55.9 us  [local(): pl.pallas_call(functools.partial(layer_kernel, n, slots, m, coupling, 1.0...]
where the time goes in v4:
time: 68.8 us; the launch traced here: 68.4 us
  Pallas kernels  55.9 us (81%)
  local copies, waits for them, and re-layouts  7.85 us (11%)
  other arithmetic  2.72 us (4%)
  matrix products  1.19 us (2%)
  between operations  0.74 us (1%)
    pallas_call x1, Pallas kernels, local(): pl.pallas_call(functools.partial(layer_kernel, n, slots, m, coupling, 1.0...  55.9 us
    unnamed x21, local copies, waits for them, and re-layouts  5.35 us

profile of v4, /device:TPU:0, one launch (start us, length us, event | category | flops | bytes accessed | tf_op | source)
XLA Modules:
  0.0 68.4 jit_solution(1502005893284031627)
XLA Ops:
  0.7 0.1 pad.18.clone
  0.7 0.0 copy-start.5
  0.7 0.6 copy-done.5
  1.4 0.0 copy-start.3
  1.4 0.1 fusion.9
  1.5 0.1 or_select_fusion
  1.5 0.5 copy-done.3
  2.1 0.0 copy-start.4
  2.1 0.6 power_multiply_fusion.decay_ref
  2.7 0.1 copy-done.4
  2.8 0.0 copy-start.2
  2.8 1.0 %fusion.10 = f32[16,256]{1,0:T(8,128)S(1)} fusion(bf16[128,16]{0,1:T(8,128)(2,1)S(1)} %copy-done.4, bf16[256,128]{1,0:T(8,128)(2,1)} %param.12), kind=kOutput, calls=%fused_computation.35 | convolution fusion | flops 1048576 | bytes 86016 | tf_op jit(solution)/shard_map/dot_general | solution.py:24
  3.8 0.7 %maximum_maximum_fusion.data_ref = f32[24,256]{1,0:T(8,128)} fusion(f32[3,256]{1,0:T(4,128)S(1)} %copy-done.3, f32[16,256]{1,0:T(8,128)S(1)} %fusion.10, f32[24]{0:T(128)S(1)} %pad.18.clone), kind=kLoop, calls=%fused_computation.12 | loop fusion | flops 12288 | bytes 44128 | tf_op jit(solution)/shard_map/concatenate | solution.py:277
  4.5 0.0 copy-start.6
  4.5 0.7 %copy.20.proj_ref = bf16[128,16]{1,0:T(8,128)(2,1)} copy(bf16[128,16]{0,1:T(8,128)(2,1)S(1)} %copy-done.4) | data formatting | bytes 8192 | tf_op args[6]
  5.2 0.0 copy-done.2
  5.2 0.0 copy-done.6
  5.2 0.1 copy.17
  5.3 0.0 copy-start.7
  5.3 0.8 %reshape.67.idx_ref = s32[8,1,2048]{2,1,0:T(1,128)} reshape(s32[256,64]{1,0:T(8,128)S(1)} %copy.17) | data formatting | bytes 131072 | tf_op jit(solution)/shard_map/reshape | solution.py:288
  6.1 0.0 copy-done.7
  6.1 0.0 copy-start.1
  6.1 0.7 %copy.21.eproj_ref = f32[128,1]{1,0:T(8,128)} copy(f32[128,1]{0,1:T(1,128)S(1)} %bitcast.14) | data formatting | bytes 1024 | tf_op jit(solution)/shard_map/broadcast_in_dim | solution.py:292
  6.8 0.1 copy-done.1
  6.9 0.1 copy.16
  7.1 0.1 reshape.66
  7.2 0.6 copy.23
  7.8 0.0 copy-start
  7.8 0.2 fusion
  8.0 0.4 copy-done
  8.4 0.6 pad_maximum_fusion.sent_ref
  9.1 0.7 fusion.1.pick_ref
  9.7 55.9 %layer.1 = (bf16[256,128]{1,0:T(8,128)(2,1)}, f32[3,256]{1,0:T(4,128)}) custom-call(bf16[2,160,128]{2,1,0:T(8,128)(2,1)} %pad_maximum_fusion.sent_ref, bf16[160,256]{1,0:T(8,128)(2,1)} %copy-done, f32[24,256]{1,0:T(8,128)} %maximum_maximum_fusion.data_ref, s32[8,1,2048]{2,1,0:T(1,128)} %reshape.67.idx_ref, bf16[8,24,32]{2,1,0:T(8,128)(2,1)} %bitcast.13, ...), custom_call_target="tpu_custom_call" | custom-call | tf_op jit(solution)/shard_map/layer/pallas_call | solution.py:296
  65.7 1.3 %copy.30 = f32[3,256]{1,0:T(4,128)} copy(f32[3,256]{1,0:T(4,128)} %get-tuple-element.21) | data formatting | bytes 6144
  67.0 1.5 %copy.31 = bf16[256,128]{1,0:T(8,128)(2,1)} copy(bf16[256,128]{1,0:T(8,128)(2,1)} %get-tuple-element.22) | data formatting | bytes 131072
  (12 shorter events, 0.1 us)
Async XLA Ops:
  0.7 0.7 copy-start.5
  1.4 0.7 %copy-start.3 = (f32[3,256]{1,0:T(4,128)S(1)}, f32[3,256]{1,0:T(4,128)}, u32[]{:S(2)}) copy-start(f32[3,256]{1,0:T(4,128)} %param.11) | copy-start | bytes 9220
  2.1 0.7 %copy-start.4 = (bf16[128,16]{0,1:T(8,128)(2,1)S(1)}, bf16[128,16]{0,1:T(8,128)(2,1)}, u32[]{:S(2)}) copy-start(bf16[128,16]{0,1:T(8,128)(2,1)} %param.16) | copy-start | bytes 12292
  2.8 2.4 %copy-start.2 = (s32[256,64]{0,1:T(8,128)S(1)}, s32[256,64]{0,1:T(8,128)}, u32[]{:S(2)}) copy-start(s32[256,64]{0,1:T(8,128)} %param.13) | copy-start | bytes 196612
  4.5 0.7 %copy-start.6 = (s32[256]{0:T(256)S(1)}, s32[256]{0:T(256)}, u32[]{:S(2)}) copy-start(s32[256]{0:T(256)} %param.14) | copy-start | bytes 3076
  5.3 0.8 %copy-start.7 = (f32[128]{0:T(128)S(1)}, f32[128]{0:T(128)}, u32[]{:S(2)}) copy-start(f32[128]{0:T(128)} %param.20) | copy-start | bytes 1540
  6.1 0.8 %copy-start.1 = (bf16[256,128]{1,0:T(8,128)(2,1)S(1)}, bf16[256,128]{1,0:T(8,128)(2,1)}, u32[]{:S(2)}) copy-start(bf16[256,128]{1,0:T(8,128)(2,1)} %param.12) | copy-start | bytes 196612
  7.8 0.6 copy-start
